TPU v7x, 128 devices: a whole 4x4x4 slice. The times are simulated.
128 devices in a mesh: dp: 32 (over z, y, core), group: 4 (over x).
Axes of the slice: x: 4, y: 4, z: 4, core: 2. Of those that a mesh axis runs over, the one named last changes fastest.
Arguments:
- hidden_in: bfloat16 [256, 128, 1024], P(('dp', 'group')), may hold values from -6 to 6
- out_grad: bfloat16 [256, 128, 1024], P(('dp', 'group')), may hold values from -6 to 6
- seq_owner: int32 [160], replicated, may hold values from 0 to 127, as said below
- token_place: int32 [256, 128], P(('dp', 'group')), may hold values from 0 to 4603, as said below
- matrix_slot: int32 [7], replicated, may hold values from 0 to 7, as said below
- weight_slots: float32 [8, 1024, 3072], P('group', 'dp'), may hold values from -1 to 1
- momentum_slots: float32 [8, 1024, 3072], P('group', 'dp'), may hold values from -448 to 448
- gains: float32 [2304], replicated, may hold values from 0.8 to 6
- gain_momentum: float32 [2304], replicated, may hold values from -448 to 448
Outputs:
- hidden_out: bfloat16 [256, 128, 1024], P(('dp', 'group'))
- in_grad: float32 [256, 128, 1024], P(('dp', 'group'))
- weight_grad: float32 [8, 1024, 3072], P('group', 'dp')
- momentum_new: float32 [8, 1024, 3072], P('group', 'dp')
- weight_new: float32 [8, 1024, 3072], P('group', 'dp')
- gain_grad: float32 [2304], replicated
- gain_momentum_new: float32 [2304], replicated
- gain_new: float32 [2304], replicated
Inputs may be any that keep to these rules, and one draw needn't show every extreme that they name: `seq_owner`: not falling; each replica is named 1 or 2 times, exactly 32 of them 2 times; a replica's sequences fill its first slots. `token_place`: strictly rising along each slot's tokens, by 1 to 4 from one token to the next. `matrix_slot`: seven distinct slots, for the query, key, value, output, gate, up and down projections in this order; slot s belongs to group index s // 2.
All inputs are finite; a program needn't handle non-finite values.
Results may differ from a plain program's by a relative error of at most 0.029.
Values may be sent and summed in bfloat16 or wider, within the bound.
No kernel may reach another device: no remote copies, remote signals or barrier semaphores. Data moves between devices by JAX's collectives and lax.ppermute only.
A program may use at most 320 MiB of HBM per device.

v0:
```python
import functools

import jax
import jax.numpy as jnp
from jax import lax
from jax.experimental import pallas as pl
from jax.experimental.pallas import tpu as pltpu
from jax.sharding import Mesh
from jax.sharding import PartitionSpec as P

D = 1024
HEADS = 16
KV = 8
HD = 128
FF = 3072
SEQ = 128
NS_ITERS = 5
WIDTHS = (HEADS * HD, KV * HD, KV * HD, HEADS * HD, FF, FF, FF)
DP_GROUP = ("dp_0", "dp_1", "dp_2", "group")
LOW = jnp.bfloat16
F32 = jnp.float32

norm_eps = 1e-06
frob_eps = 1e-07
rope_base = 1000000.0
coef_linear = 3.4445
coef_square = -4.775
coef_quartic = 2.0315
momentum_keep = 0.95
learn_rate = 0.15
weight_decay = 0.1
gain_rate = 0.5
masked_score = -1e30
score_scale = HD ** (-0.5)

NEAR = ((0, 1), (1, 0), (2, 3), (3, 2))
FAR = ((0, 3), (3, 0), (1, 2), (2, 1))
LINKS = (("dp_0", NEAR), ("dp_1", NEAR), ("dp_0", FAR), ("dp_1", FAR))
MASKS = (0, 3, 1, 2)


def place_of(mask):
    return jnp.where(mask == 0, 0, jnp.where(mask == 3, 1, mask + 1))


def swap(x):
    return lax.ppermute(x, "dp_2", ((0, 1), (1, 0)))


def together(arrays):
    return list(lax.optimization_barrier(tuple(arrays)))


def gather_came(quarters, step):
    fresh = []
    for i in range(4):
        axis, pairs = LINKS[(step + i) % 4]
        fresh.append(lax.ppermute(quarters[i], axis, pairs))
    return together(fresh)


def gather_step(quarters, step):
    fresh = gather_came(quarters, step)
    return [
        jnp.concatenate([quarters[i], fresh[i]], axis=(step + i) % 4) for i in range(4)
    ]


def gather_shaped(x, width):
    return [
        x[:, i * width : (i + 1) * width].reshape(1, 1, 1, 1, x.shape[0], width) for i in range(4)
    ]


def flat(quarters):
    return [q.reshape(-1, q.shape[-1]) for q in quarters]


def scatter_step(sent, kept, step):
    to_send, to_keep, came = [], [], []
    for i in range(4):
        axis, pairs = LINKS[(step + i) % 4]
        came.append(lax.ppermute(sent[i], axis, pairs))
    came = together(came)
    for i in range(4):
        at = (step + 1 + i) % 4

        def half(part):
            if step == 3:
                return (kept[i].astype(F32) + came[i].astype(F32)).astype(LOW)
            both_parts = [lax.slice_in_dim(x, part, part + 1, axis=at) for x in (kept[i], came[i])]
            return (both_parts[0].astype(F32) + both_parts[1].astype(F32)).astype(LOW)

        to_keep.append(half(0))
        if step < 3:
            to_send.append(half(1))
    return to_send, to_keep


def gather_group(halves, after):
    held = [h[None, None] for h in halves]
    for step in range(2):
        fresh = [lax.ppermute(held[i], "group", (NEAR, FAR)[(step + i) % 2]) for i in range(2)]
        if step == 0:
            *fresh, after = together([*fresh, after])
        held = [jnp.concatenate([held[i], fresh[i]], axis=(step + i) % 2) for i in range(2)]
    return [h.reshape(8, *h.shape[3:]) for h in held], after


def dot(left, right, dims=((1,), (0,))):
    return lax.dot_general(left, right, (dims, ((), ())), preferred_element_type=F32)


ROWS = ((0,), (0,))
LAST = ((1,), (1,))
PLAIN = ((1,), (0,))


def split_two(x):
    high = lax.reduce_precision(x, exponent_bits=8, mantissa_bits=7)
    return high.astype(LOW), (x - high).astype(LOW)


def half_turn(u):
    return jnp.concatenate([u[:, HD // 2 :], u[:, : HD // 2]], axis=1)


def head_forward(raw, gain, cosine, sine):
    scale = lax.rsqrt(jnp.mean(raw * raw, axis=-1, keepdims=True) + norm_eps)
    normed = raw * scale
    gained = normed * gain
    turned = gained * cosine + half_turn(gained) * sine
    return normed, scale, turned.astype(LOW)


def softmax_parts(query, key):
    scores = dot(query, key, LAST) * score_scale
    rows = lax.broadcasted_iota(jnp.int32, scores.shape, 0) & (SEQ - 1)
    columns = lax.broadcasted_iota(jnp.int32, scores.shape, 1)
    scores = jnp.where(rows >= columns, scores, masked_score)
    terms = jnp.exp(scores - jnp.max(scores, axis=-1, keepdims=True))
    return terms / jnp.sum(terms, axis=-1, keepdims=True)


def two_heads(ref, at):
    return jnp.concatenate([ref[at, :HD], ref[at, HD : 2 * HD]], axis=0)


def twice(x):
    return jnp.concatenate([x, x], axis=0)


def heads_kernel(
    input_ref, weight_ref, cos_ref, sin_ref, gain_ref, sum_ref, raw_ref, attn_ref, out_ref
):
    raw_ref[...] = dot(input_ref[...], weight_ref[:, : 4 * HD])
    for b in range(raw_ref.shape[0] // SEQ):
        at = slice(b * SEQ, (b + 1) * SEQ)
        cosine, sine = cos_ref[at, :], sin_ref[at, :]
        _, _, key = head_forward(raw_ref[at, 2 * HD : 3 * HD], gain_ref[1:2, :], cosine, sine)
        value = raw_ref[at, 3 * HD :].astype(LOW)
        _, _, query = head_forward(
            two_heads(raw_ref, at), gain_ref[0:1, :], twice(cosine), twice(sine)
        )
        probs = softmax_parts(query, key).astype(LOW)
        out = dot(probs, value).astype(LOW)
        attn_ref[at, :HD] = out[:SEQ]
        attn_ref[at, HD:] = out[SEQ:]
    out_ref[...] = sum_ref[...] + dot(attn_ref[...], weight_ref[:, 4 * HD :], LAST)


def head_backward(grad, normed, scale, gain, cosine, sine):
    back = grad * cosine - half_turn(grad) * sine
    term = jnp.sum(back * normed, axis=0, keepdims=True)
    g = back * gain
    raw = scale * (g - normed * jnp.mean(g * normed, axis=-1, keepdims=True))
    return raw.astype(LOW), term


def heads_back_kernel(
    raw_ref,
    branch_ref,
    weight_ref,
    cos_ref,
    sin_ref,
    gain_ref,
    sum_ref,
    out_ref,
    term_ref,
    one_ref,
    grad_ref,
):
    grad_ref[...] = dot(branch_ref[...], weight_ref[:, 4 * HD :]).astype(LOW)
    query_terms, key_terms = 0.0, 0.0
    for b in range(raw_ref.shape[0] // SEQ):
        at = slice(b * SEQ, (b + 1) * SEQ)
        cosine, sine = cos_ref[at, :], sin_ref[at, :]
        cosines, sines = twice(cosine), twice(sine)
        key_hat, key_scale, key = head_forward(
            raw_ref[at, 2 * HD : 3 * HD], gain_ref[1:2, :], cosine, sine
        )
        value = raw_ref[at, 3 * HD :].astype(LOW)
        query_hat, query_scale, query = head_forward(
            two_heads(raw_ref, at), gain_ref[0:1, :], cosines, sines
        )
        probs = softmax_parts(query, key)
        grad_attn = two_heads(grad_ref, at)
        grad_value = dot(probs.astype(LOW), grad_attn, ROWS)
        grad_probs = dot(grad_attn, value, LAST)
        inner = jnp.sum(probs * grad_probs, axis=-1, keepdims=True)
        grad_scores = (probs * (grad_probs - inner)).astype(LOW)
        grad_query = dot(grad_scores, key) * score_scale
        grad_key = dot(grad_scores, query, ROWS) * score_scale
        raw, term = head_backward(
            grad_query, query_hat, query_scale, gain_ref[0:1, :], cosines, sines
        )
        query_terms = query_terms + term
        out_ref[at, :HD] = raw[:SEQ]
        out_ref[at, HD : 2 * HD] = raw[SEQ:]
        raw, term = head_backward(grad_key, key_hat, key_scale, gain_ref[1:2, :], cosine, sine)
        key_terms = key_terms + term
        out_ref[at, 2 * HD : 3 * HD] = raw
        out_ref[at, 3 * HD :] = grad_value.astype(LOW)
    spare = jnp.zeros((6, HD), F32)
    term_ref[...] = jnp.concatenate([query_terms, key_terms, spare], axis=0)
    one_ref[...] = sum_ref[...] + dot(out_ref[...], weight_ref[:, : 4 * HD], LAST)


BLOCK = D // 4


def iterate_kernel(*refs):
    pieces, out_ref, refs = refs[:8], refs[8], refs[9:]
    quarters, gram, high, low, poly, mixed_high, mixed_low, own, arrived = refs[:4], *refs[4:]
    copies = []
    for i in range(4):
        for part in range(2):
            place = [slice(None)] * 4
            place[(3 + i) % 4] = slice(part, part + 1)
            copies.append(
                pltpu.make_async_copy(
                    pieces[2 * i + part], quarters[i].at[tuple(place)], arrived.at[2 * i + part]
                )
            )
    for copy in copies:
        copy.start()
    for copy in copies:
        copy.wait()
    x0, x1, x2, x3 = [q.reshape(D, q.shape[-1]) for q in quarters]
    at = [slice(i * BLOCK, (i + 1) * BLOCK) for i in range(4)]
    blocks = [(i, j) for i in range(4) for j in range(4)]

    def parts(x):
        top = x.astype(LOW)
        return top, (x - top.astype(F32)).astype(LOW)

    def mirrored(ref, i, j, block):
        ref[at[i], at[j]] = block.astype(ref.dtype)
        if i != j:
            ref[at[j], at[i]] = block.T.astype(ref.dtype)

    def two_dot(left, right):
        rows = left.shape[0]
        both_parts = dot(jnp.concatenate(parts(left), axis=0), right)
        return both_parts[:rows] + both_parts[rows:]

    rows = lax.broadcasted_iota(jnp.int32, (BLOCK, BLOCK), 0)
    columns = lax.broadcasted_iota(jnp.int32, (BLOCK, BLOCK), 1)
    trace = jnp.zeros((1, 1), F32)
    for i, j in blocks:
        if j > i:
            continue
        block = sum(
            dot(x[at[i], : FF // 4], x[at[j], : FF // 4], LAST) for x in (x0, x1, x2, x3)
        )
        mirrored(gram, i, j, block)
        if i == j:
            diagonal = jnp.where(rows == columns, block, 0.0)
            trace = trace + jnp.sum(jnp.sum(diagonal, axis=1, keepdims=True), axis=0, keepdims=True)
    inverse = 1.0 / (jnp.sqrt(trace) + frob_eps)
    for i, j in blocks:
        block = gram[at[i], at[j]] * (inverse * inverse)
        gram[at[i], at[j]] = block
        high[at[i], at[j]], low[at[i], at[j]] = parts(block)
    own_rows = lax.broadcasted_iota(jnp.int32, own.shape, 0)
    own[...] = (own_rows == lax.broadcasted_iota(jnp.int32, own.shape, 1)).astype(F32)

    def set_poly():
        for i, j in blocks:
            if j > i:
                continue
            square = dot(high[at[i], :], high[:, at[j]])
            block = coef_square * high[at[i], at[j]].astype(F32) + coef_quartic * square
            mirrored(poly, i, j, block)

    def through_poly(x):
        return coef_linear * x + two_dot(x, poly[...])

    def sweep(_, carry):
        set_poly()
        own[...] = through_poly(own[...])
        for i, j in blocks:
            block = dot(high[at[i], :], poly[:, at[j]]) + dot(low[at[i], :], poly[:, at[j]])
            gram[at[i], at[j]] = (coef_linear * coef_linear) * gram[at[i], at[j]] + (
                2.0 * coef_linear
            ) * block
            mixed_high[at[i], at[j]], mixed_low[at[i], at[j]] = parts(block)
        for i, j in blocks:
            block = dot(mixed_high[at[i], :], poly[:, at[j]])
            block = block + dot(mixed_low[at[i], :], poly[:, at[j]]) + gram[at[i], at[j]]
            gram[at[i], at[j]] = block
            high[at[i], at[j]], low[at[i], at[j]] = parts(block)
        return carry

    lax.fori_loop(0, NS_ITERS - 2, sweep, 0)
    set_poly()
    own[...] = through_poly(own[...])

    def through_next(x):
        x = through_poly(x)
        x = two_dot(x, high[...]) + dot(x.astype(LOW), low[...])
        return through_poly(x)

    once = through_next(own[...])
    second = through_next(once)
    last = coef_linear * own[...] + coef_square * once + coef_quartic * second
    last = last * inverse
    for k, x in enumerate((x0, x1, x2, x3)):
        width = FF // 4
        out_ref[:, k * width : (k + 1) * width] = two_dot(last, x[:, :width]).astype(LOW)


def iterate_rows(pieces):
    square = pltpu.VMEM((D, D), LOW)
    quarters = [pltpu.VMEM((2, 2, 2, 2, D // 16, x.shape[-1]), LOW) for x in pieces[::2]]
    return pl.pallas_call(
        iterate_kernel,
        in_specs=[pl.BlockSpec(memory_space=pl.ANY)] * 8,
        out_specs=pl.BlockSpec(memory_space=pltpu.VMEM),
        out_shape=jax.ShapeDtypeStruct((64, FF), LOW),
        scratch_shapes=[
            *quarters,
            pltpu.VMEM((D, D), F32),
            *[square] * 5,
            pltpu.VMEM((64, D), F32),
            pltpu.SemaphoreType.DMA((8,)),
        ],
        compiler_params=pltpu.CompilerParams(vmem_limit_bytes=48 * 2**20),
        cost_estimate=pl.CostEstimate(flops=50 * 10**9, bytes_accessed=2**23, transcendentals=0),
    )(*pieces)


def by_sequence(width):
    return pl.BlockSpec((2 * SEQ, width), lambda s: (s, 0))


def whole(rows, width):
    return pl.BlockSpec((rows, width), lambda s: (0, 0))


SMALL = pl.CostEstimate(flops=2**20, bytes_accessed=2**16, transcendentals=0)
KERNEL_SPACE = pltpu.CompilerParams(vmem_limit_bytes=32 * 2**20)


def heads_forward(inputs, weight, cosine, sine, gain_rows, total):
    tokens = inputs.shape[0]
    return pl.pallas_call(
        heads_kernel,
        grid=(tokens // (2 * SEQ),),
        in_specs=[
            by_sequence(D),
            whole(D, 6 * HD),
            by_sequence(HD),
            by_sequence(HD),
            whole(8, HD),
            by_sequence(D),
        ],
        out_specs=[by_sequence(4 * HD), by_sequence(2 * HD), by_sequence(D)],
        out_shape=[
            jax.ShapeDtypeStruct((tokens, 4 * HD), F32),
            jax.ShapeDtypeStruct((tokens, 2 * HD), LOW),
            jax.ShapeDtypeStruct((tokens, D), F32),
        ],
        compiler_params=KERNEL_SPACE,
        cost_estimate=SMALL,
    )(inputs, weight, cosine, sine, gain_rows, total)


def heads_backward(raw, branch, weight, cosine, sine, gain_rows, total):
    tokens = raw.shape[0]
    grad_raw, terms, total = pl.pallas_call(
        heads_back_kernel,
        grid=(tokens // (2 * SEQ),),
        in_specs=[
            by_sequence(4 * HD),
            by_sequence(D),
            whole(D, 6 * HD),
            by_sequence(HD),
            by_sequence(HD),
            whole(8, HD),
            by_sequence(D),
        ],
        out_specs=[
            by_sequence(4 * HD),
            pl.BlockSpec((8, HD), lambda s: (s, 0)),
            by_sequence(D),
        ],
        out_shape=[
            jax.ShapeDtypeStruct((tokens, 4 * HD), LOW),
            jax.ShapeDtypeStruct((tokens // (2 * SEQ) * 8, HD), F32),
            jax.ShapeDtypeStruct((tokens, D), F32),
        ],
        scratch_shapes=[pltpu.VMEM((2 * SEQ, 2 * HD), LOW)],
        compiler_params=KERNEL_SPACE,
        cost_estimate=SMALL,
    )(raw, branch, weight, cosine, sine, gain_rows, total)
    return grad_raw, jnp.sum(terms.reshape(-1, 8, HD), axis=0), total


def inner_kernel(
    input_ref, grad_ref, w0, w1, w2, w3, act_ref, inner_ref, outward_ref, back_ref
):
    width = FF // 8
    outward, back = 0.0, 0.0
    for i, w in enumerate((w0, w1, w2, w3)):
        gate_up = dot(input_ref[...], w[:, : 2 * width])
        gate, up = gate_up[:, :width], gate_up[:, width:]
        sigmoid = jax.nn.sigmoid(gate)
        swish = gate * sigmoid
        act = (swish * up).astype(LOW)
        act_ref[:, i * width : (i + 1) * width] = act
        grad_act = dot(grad_ref[...], w[:, 2 * width :])
        slope = sigmoid * (1.0 + gate * (1.0 - sigmoid))
        start = i * 2 * width
        inner_ref[:, start : start + width] = (grad_act * up * slope).astype(LOW)
        inner_ref[:, start + width : start + 2 * width] = (grad_act * swish).astype(LOW)
        outward = outward + dot(act, w[:, 2 * width :], LAST)
        back = back + dot(inner_ref[:, start : start + 2 * width], w[:, : 2 * width], LAST)
    outward_ref[...] = outward
    back_ref[...] = back


def inner_units(inputs, grads, weights):
    tokens = inputs.shape[0]
    return pl.pallas_call(
        inner_kernel,
        in_specs=[pl.BlockSpec(memory_space=pltpu.VMEM)] * 6,
        out_specs=[pl.BlockSpec(memory_space=pltpu.VMEM)] * 4,
        out_shape=[
            jax.ShapeDtypeStruct((tokens, FF // 2), LOW),
            jax.ShapeDtypeStruct((tokens, FF), LOW),
            jax.ShapeDtypeStruct((tokens, D), F32),
            jax.ShapeDtypeStruct((tokens, D), F32),
        ],
        compiler_params=pltpu.CompilerParams(vmem_limit_bytes=48 * 2**20),
        cost_estimate=SMALL,
    )(inputs, grads, *weights)


def terms_kernel(link, first_left, first_right, second_left, second_right, kept_ref, sent_ref):
    width = first_right.shape[1]
    first = dot(first_left[...], first_right[...], ROWS).astype(LOW)
    second = dot(second_left[...], second_right[...], ROWS).astype(LOW)

    def put(ref, to, start, rows):
        ref[to : to + rows, :width] = first[start : start + rows]
        ref[to : to + rows, width:] = second[start : start + rows]

    if link < 2:
        block = pl.program_id(0)
        part = block // 2 if link == 0 else block % 2

        @pl.when(part == 0)
        def _():
            put(kept_ref, 0, 0, BLOCK)

        @pl.when(part == 1)
        def _():
            put(sent_ref, 0, 0, BLOCK)

    else:
        rows = 128 if link == 2 else 64
        for start in range(0, BLOCK, 2 * rows):
            put(kept_ref, start // 2, start, rows)
            put(sent_ref, start // 2, start + rows, rows)


def terms(link, first_left, first_right, second_left, second_right):
    tokens = first_left.shape[0]

    def right(x, at, width):
        return x, pl.BlockSpec((tokens, width), lambda r: (0, at))

    left = pl.BlockSpec((tokens, BLOCK), lambda r: (0, r))
    operands = [(first_left, left), right(*first_right), (second_left, left), right(*second_right)]
    width = first_right[2] + second_right[2]
    if link == 0:
        specs = [
            pl.BlockSpec((BLOCK, width), lambda r: (jnp.minimum(r, 1), 0)),
            pl.BlockSpec((BLOCK, width), lambda r: (jnp.maximum(r - 2, 0), 0)),
        ]
    elif link == 1:
        specs = [pl.BlockSpec((BLOCK, width), lambda r: (r // 2, 0))] * 2
    else:
        specs = [pl.BlockSpec((BLOCK // 2, width), lambda r: (r, 0))] * 2
    half = jax.ShapeDtypeStruct((D // 2, width), LOW)
    kept, sent = pl.pallas_call(
        functools.partial(terms_kernel, link),
        grid=(4,),
        in_specs=[spec for _, spec in operands],
        out_specs=specs,
        out_shape=[half, half],
        compiler_params=KERNEL_SPACE,
        cost_estimate=SMALL,
    )(*[x for x, _ in operands])
    shape = [2, 2, 2, 2, D // 16, width]
    shape[link] = 1
    return kept.reshape(shape), sent.reshape(shape)


def shared_sum(partial):
    own = partial.shape[0] // 2
    return partial[:own] + swap(partial[own:].astype(LOW)).astype(F32)


def both(x):
    return jnp.concatenate([x, swap(x)], axis=0)


def norm_back(grad_hat, normed, scale):
    return scale * (grad_hat - normed * jnp.mean(grad_hat * normed, axis=-1, keepdims=True))


HEADS_WIDTH, INNER_WIDTH = 6 * HD, 3 * FF // 8


def pieces_of(core):
    pieces = []
    for i in range(core * 4, core * 4 + 4):
        pieces += [(0, i * 2 * HD, 2 * HD), (1, i * HD, HD), (2, i * HD, HD), (3, i * 2 * HD, 2 * HD)]
    for i in range(core * 4, core * 4 + 4):
        pieces += [(m, i * FF // 8, FF // 8) for m in (4, 5, 6)]
    return pieces


HALF_WIDTH = sum(WIDTHS) // 2


def compact_kernel(at_ref, top_ref, low_ref, mine_ref, theirs_ref):
    for core in range(2):

        @pl.when(at_ref[7] == core)
        def _():
            for out_ref, pieces in ((mine_ref, pieces_of(core)), (theirs_ref, pieces_of(1 - core))):
                to = 0
                for m, start, width in pieces:
                    out_ref[:16, to : to + width] = top_ref[at_ref[m], :, start : start + width]
                    out_ref[16:, to : to + width] = low_ref[at_ref[m], :, start : start + width]
                    to += width


def compact(at, top, low):
    half = jax.ShapeDtypeStruct((32, HALF_WIDTH), LOW)
    in_vmem = pl.BlockSpec(memory_space=pltpu.VMEM)
    return pl.pallas_call(
        compact_kernel,
        in_specs=[pl.BlockSpec(memory_space=pltpu.SMEM), in_vmem, in_vmem],
        out_specs=[in_vmem, in_vmem],
        out_shape=[half, half],
        compiler_params=pltpu.CompilerParams(vmem_limit_bytes=24 * 2**20),
        cost_estimate=pl.CostEstimate(flops=0, bytes_accessed=5 * 2**20, transcendentals=0),
    )(at, top, low)


def route_kernel(of_ref, kept_ref, got_ref, top_keep, top_send, low_keep, low_send, held):
    held[...] = jnp.zeros_like(held)
    for core in range(2):

        @pl.when(of_ref[8] == core)
        def _():
            for in_ref, pieces in ((kept_ref, pieces_of(core)), (got_ref, pieces_of(1 - core))):
                at = 0
                for m, start, width in pieces:
                    held[m, :, start : start + width] = in_ref[:, at : at + width]
                    at += width

    for place in range(8):
        near, far, j = place // 4, (place // 2) % 2, place % 2
        (top_keep, top_send)[near][2 * far + j] = held[of_ref[place], :16, :]
        (low_keep, low_send)[far][2 * near + j] = held[of_ref[place], 16:, :]


def route(of, kept, got):
    half = jax.ShapeDtypeStruct((4, 16, FF), LOW)
    in_vmem = pl.BlockSpec(memory_space=pltpu.VMEM)
    return pl.pallas_call(
        route_kernel,
        in_specs=[pl.BlockSpec(memory_space=pltpu.SMEM), in_vmem, in_vmem],
        out_specs=[in_vmem] * 4,
        out_shape=[half] * 4,
        scratch_shapes=[pltpu.VMEM((8, 32, FF), LOW)],
        compiler_params=pltpu.CompilerParams(vmem_limit_bytes=24 * 2**20),
        cost_estimate=pl.CostEstimate(flops=0, bytes_accessed=5 * 2**20, transcendentals=0),
    )(of, kept, got)


def shards(
    hidden_in,
    out_grad,
    seq_owner,
    token_place,
    matrix_slot,
    weight_slots,
    momentum_slots,
    gains,
    gain_momentum,
):
    slot_count, length = hidden_in.shape[:2]
    tok_count = slot_count * length
    z, y = lax.axis_index("dp_0"), lax.axis_index("dp_1")
    core, group = lax.axis_index("dp_2"), lax.axis_index("group")
    first_core = core == 0
    replica = ((z * 4 + y) * 2 + core) * 4 + group

    def core_pick(zero, one):
        return jnp.where(first_core, zero, one)

    weight_low = weight_slots.astype(LOW)
    (slots_top, slots_low), hidden_in = gather_group(
        [weight_low[:, :16], weight_low[:, 16:]], hidden_in
    )
    at = place_of(jnp.bitwise_xor(group, matrix_slot >> 1)) * 2 + (matrix_slot & 1)
    mine, theirs = compact(jnp.concatenate([at, core[None]]), slots_top, slots_low)
    got = swap(theirs)
    chip_rows = core_pick(
        jnp.concatenate([mine, got], axis=0), jnp.concatenate([got, mine], axis=0)
    )
    heads_held = gather_shaped(chip_rows[:, : 4 * HEADS_WIDTH], HEADS_WIDTH)
    inner_held = gather_shaped(chip_rows[:, 4 * HEADS_WIDTH :], INNER_WIDTH)
    column = lax.broadcasted_iota(jnp.int32, (D, D), 1)
    source = lax.broadcasted_iota(jnp.int32, (D, D), 0)
    block = column // 64
    near_z, near_y = block // 8, (block // 4) % 2
    far_z, far_y = (block // 2) % 2, block % 2
    from_z = jnp.bitwise_xor(z, jnp.bitwise_xor(near_z, far_z * 3))
    from_y = jnp.bitwise_xor(y, jnp.bitwise_xor(near_y, far_y * 3))
    reorder = (source == (from_z * 4 + from_y) * 64 + column % 64).astype(LOW)

    live_count = jnp.sum((seq_owner == replica).astype(jnp.int32))
    live_slot = (jnp.arange(slot_count, dtype=jnp.int32) < live_count).astype(F32)
    live_token = jnp.repeat(live_slot, length)[:, None]
    tokens = dot(hidden_in.reshape(tok_count, D), reorder)
    grad_out = dot(out_grad.reshape(tok_count, D), reorder) * live_token
    grad_low = both(grad_out.astype(LOW))
    layer_gains = jnp.dot(
        gains[: 2 * D].reshape(2, D), reorder.astype(F32), precision=lax.Precision.HIGHEST
    )
    gain_one, gain_two = layer_gains[0:1], layer_gains[1:2]
    gain_rows = jnp.pad(gains[2 * D :].reshape(2, HD), ((0, 6), (0, 0)))
    places = both(token_place).astype(F32).reshape(-1, 1)
    exponent = jnp.arange(HD // 2, dtype=F32) * (-2.0 / HD)
    angles = places * jnp.power(rope_base, exponent)[None, :]
    cosine, sine = jnp.cos(angles), jnp.sin(angles)
    cosine = jnp.concatenate([cosine, cosine], axis=1)
    sine = jnp.concatenate([-sine, sine], axis=1)

    scale_one = lax.rsqrt(jnp.mean(tokens * tokens, axis=-1, keepdims=True) + norm_eps)
    normed_one = tokens * scale_one
    input_one = both((normed_one * gain_one).astype(LOW))
    heads_held = together(gather_step(heads_held, 0))
    held = together([*gather_step(heads_held, 1), *gather_step(inner_held, 0)])
    held = together([*gather_step(held[:4], 2), *gather_step(held[4:], 1)])
    held = together([*gather_step(held[:4], 3), *gather_step(held[4:], 2)])
    w_heads = flat(held[:4])
    w_inner = flat(gather_step(held[4:], 3))
    raw, attn = [], []
    branch = jnp.zeros((2 * tok_count, D), F32)
    for w in w_heads:
        fresh, heads, branch = heads_forward(input_one, w, cosine, sine, gain_rows, branch)
        raw.append(fresh)
        attn.append(heads)
    *w_inner, branch = together([*w_inner, branch])
    residual = tokens + shared_sum(branch)
    scale_two = lax.rsqrt(jnp.mean(residual * residual, axis=-1, keepdims=True) + norm_eps)
    normed_two = residual * scale_two
    input_two = both((normed_two * gain_two).astype(LOW))
    act, grad_inner, outward, grad_two = inner_units(input_two, grad_low, w_inner)
    result = (residual + shared_sum(outward)) * live_token
    hidden_out = dot(result.astype(LOW), reorder, LAST).astype(LOW)

    sent, kept = [], []
    for i in range(4):
        keep, send = terms(
            i, input_two, (grad_inner, i, FF // 4), grad_low, (act, i, FF // 8)
        )
        sent.append(send)
        kept.append(keep)
    grad_two = shared_sum(grad_two)
    gain_two_term = jnp.sum(grad_two * normed_two, axis=0, keepdims=True)
    grad_residual = grad_out + norm_back(grad_two * gain_two, normed_two, scale_two)
    branch_low = both(grad_residual.astype(LOW))
    grad_one, head_terms, grad_raw = jnp.zeros((2 * tok_count, D), F32), 0.0, []
    heads_sent, heads_kept = [], []

    def back_through(i, branch, grad_one):
        fresh, term, grad_one = heads_backward(
            raw[i], branch, w_heads[i], cosine, sine, gain_rows, grad_one
        )
        grad_raw.append(fresh)
        return head_terms + term, grad_one

    def heads_terms(i):
        keep, send = terms(
            i, input_one, (grad_raw[i], 0, 4 * HD), branch_low, (attn[i], 0, 2 * HD)
        )
        heads_kept.append(keep)
        heads_sent.append(send)

    head_terms, grad_one = back_through(0, branch_low, grad_one)
    head_terms, grad_one = back_through(1, branch_low, grad_one)
    sent, kept = scatter_step(sent, kept, 0)
    *held, branch_low, grad_one = together([*sent, *kept, branch_low, grad_one])
    sent, kept = held[:4], held[4:]
    head_terms, grad_one = back_through(2, branch_low, grad_one)
    heads_terms(0)
    sent, kept = scatter_step(sent, kept, 1)
    *held, branch_low, heads_sent[0], grad_one = together(
        [*sent, *kept, branch_low, heads_sent[0], grad_one]
    )
    sent, kept = held[:4], held[4:]
    head_terms, grad_one = back_through(3, branch_low, grad_one)
    heads_terms(1)
    sent, kept = scatter_step(sent, kept, 2)
    *held, heads_sent[1], grad_one = together([*sent, *kept, heads_sent[1], grad_one])
    sent, kept = held[:4], held[4:]
    heads_terms(2)
    heads_terms(3)
    sent, kept = scatter_step(sent, kept, 3)
    inner_sums = flat(kept)
    sent, kept = heads_sent, heads_kept
    grad_one = shared_sum(grad_one)
    gain_one_term = jnp.sum(grad_one * normed_one, axis=0, keepdims=True)
    in_grad = grad_residual + norm_back(grad_one * gain_one, normed_one, scale_one)
    in_high, in_low = split_two(in_grad)
    in_grad = dot(in_high, reorder, LAST) + dot(in_low, reorder, LAST)
    layer_terms = lax.dot_general(
        jnp.concatenate([gain_one_term, gain_two_term], axis=0),
        reorder.astype(F32),
        (LAST, ((), ())),
        precision=lax.Precision.HIGHEST,
    )
    gain_sum = jnp.concatenate([layer_terms.reshape(-1), head_terms[:2].reshape(-1)])
    for step in range(4):
        sent, kept = scatter_step(sent, kept, step)
        if step == 1:
            gain_sum = gain_sum + swap(gain_sum)
        elif step > 1:
            gain_sum = gain_sum + lax.ppermute(gain_sum, "group", (NEAR, FAR)[step - 2])
        if step == 0:
            *held, in_grad, gain_sum = together([*sent, *kept, in_grad, gain_sum])
        else:
            *held, gain_sum = together([*sent, *kept, gain_sum])
        sent, kept = held[:-4], held[-4:]
    heads_sums = flat(kept)

    sums = jnp.concatenate([*heads_sums, *inner_sums], axis=1)
    kept = core_pick(sums[:32], sums[32:])
    got = swap(core_pick(sums[32:], sums[:32]))
    slot_at = (jnp.bitwise_xor(group, jnp.asarray(MASKS, jnp.int32)) * 2)[:, None]
    slot_at = (slot_at + jnp.arange(2, dtype=jnp.int32)[None, :]).reshape(8)
    matches = slot_at[:, None] == matrix_slot[None, :]
    numbers = jnp.arange(7, dtype=jnp.int32)[None, :]
    routed_from = 7 - jnp.max(jnp.where(matches, 7 - numbers, 0), axis=1)
    halves = route(jnp.concatenate([routed_from, core[None]]), kept, got)
    sent, kept = [halves[1], halves[3]], [halves[0], halves[2]]
    for step in range(2):
        got = together(
            [lax.ppermute(sent[i], "group", (NEAR, FAR)[(step + i) % 2]) for i in range(2)]
        )
        total = [kept[i].astype(F32) + got[i].astype(F32) for i in range(2)]
        if step == 0:
            held = together([*(t[2:].astype(LOW) for t in total), *(t[:2].astype(LOW) for t in total)])
            sent, kept = held[:2], held[2:]
    weight_grad = jnp.concatenate(total, axis=1)

    own_ids = group * 2 + jnp.arange(2, dtype=jnp.int32)
    own_match = own_ids[:, None] == matrix_slot[None, :]
    own_width = jnp.sum(jnp.where(own_match, jnp.asarray(WIDTHS, jnp.int32)[None, :], 0), axis=1)
    own_width = own_width.astype(jnp.int32)
    column_mask = (jnp.arange(FF, dtype=jnp.int32)[None, :] < own_width[:, None]).astype(F32)
    column_mask = column_mask[:, None, :]
    momentum_new = column_mask * (momentum_keep * momentum_slots + weight_grad)
    direction = (weight_grad + momentum_keep * momentum_new).astype(LOW)

    mine = core_pick(direction[0], direction[1])
    got = swap(core_pick(direction[1], direction[0]))
    rows = core_pick(jnp.concatenate([mine, got], axis=0), jnp.concatenate([got, mine], axis=0))
    gain_parts, rest = [], gain_sum
    for _ in range(3):
        part = lax.reduce_precision(rest, exponent_bits=8, mantissa_bits=7)
        gain_parts.append(part.astype(LOW))
        rest = rest - part
    gain_parts = jnp.pad(jnp.concatenate(gain_parts), (0, 64 * HD - 3 * gain_sum.shape[0]))
    held = gather_shaped(rows, FF // 4)
    held[0] = jnp.concatenate([held[0], gain_parts.reshape(1, 1, 1, 1, 64, HD)], axis=-1)
    for step in range(3):
        held = together(gather_step(held, step))
    fresh = gather_came(held, 3)
    pieces = [x for pair in zip(held, fresh) for x in pair]
    gain_parts = jnp.concatenate([x[..., FF // 4 :] for x in pieces[:2]], axis=3)
    gain_parts = gain_parts.reshape(16, 64 * HD)
    place = lax.broadcasted_iota(jnp.int32, (16, 16), 1)
    of_z = jnp.bitwise_xor(z, jnp.bitwise_xor(place // 8, (place // 2) % 2 * 3))
    of_y = jnp.bitwise_xor(y, jnp.bitwise_xor((place // 4) % 2, place % 2 * 3))
    in_turn = (lax.broadcasted_iota(jnp.int32, (16, 16), 0) == of_z * 4 + of_y).astype(LOW)
    gain_parts = dot(in_turn, gain_parts)[:, : 3 * gain_sum.shape[0]].reshape(16, 3, -1)
    gain_grad = jnp.sum(gain_parts[:, 0] + gain_parts[:, 1] + gain_parts[:, 2], axis=0)
    iterate = iterate_rows(pieces)
    kept = core_pick(iterate[:32], iterate[32:])
    got = swap(core_pick(iterate[32:], iterate[:32]))
    iterate = jnp.stack([core_pick(kept, got), core_pick(got, kept)]).astype(F32)
    update_scale = 0.2 * jnp.sqrt(jnp.maximum(own_width, D).astype(F32))
    weight_new = column_mask * (
        weight_slots * (1.0 - learn_rate * weight_decay)
        - learn_rate * update_scale[:, None, None] * iterate
    )

    gain_momentum_new = momentum_keep * gain_momentum + gain_grad
    gain_step = gain_grad + momentum_keep * gain_momentum_new
    bounds = (0, D, 2 * D, 2 * D + HD, 2 * D + 2 * HD)
    scaled_parts = []
    for number in range(4):
        segment = gain_step[bounds[number] : bounds[number + 1]]
        scaled_parts.append(segment * lax.rsqrt(jnp.mean(segment * segment) + norm_eps))
    gain_new = gains - gain_rate * jnp.concatenate(scaled_parts)
    shape = (slot_count, length, D)
    return (
        hidden_out.reshape(shape),
        in_grad.reshape(shape),
        weight_grad,
        momentum_new,
        weight_new,
        gain_grad,
        gain_momentum_new,
        gain_new,
    )


def solution(mesh):
    finer = Mesh(
        mesh.devices.reshape(4, 4, 2, mesh.shape["group"]), ("dp_0", "dp_1", "dp_2", "group")
    )
    in_specs = (
        P(DP_GROUP, None, None),
        P(DP_GROUP, None, None),
        P(),
        P(DP_GROUP, None),
        P(),
        P("group", ("dp_0", "dp_1", "dp_2"), None),
        P("group", ("dp_0", "dp_1", "dp_2"), None),
        P(),
        P(),
    )
    out_specs = (
        P(DP_GROUP, None, None),
        P(DP_GROUP, None, None),
        P("group", ("dp_0", "dp_1", "dp_2"), None),
        P("group", ("dp_0", "dp_1", "dp_2"), None),
        P("group", ("dp_0", "dp_1", "dp_2"), None),
        P(),
        P(),
        P(),
    )
    return jax.shard_map(
        shards, mesh=finer, in_specs=in_specs, out_specs=out_specs, check_vma=False
    )
```

profile of v0, /device:TPU:1, one launch (start us, length us, event | category | flops | bytes accessed | tf_op | source)
XLA Modules:
  0.0 460.5 jit_solution(7290841338854266751)
XLA Ops:
  12.9 6.7 %collective-permute-done.3 = bf16[1,2,2,16,3072]{4,3,2,1,0:T(8,128)(2,1)S(1)} collective-permute-done((bf16[1,2,2,16,3072]{4,3,2,1,0:T(8,128)(2,1)S(1)}, bf16[1,2,2,16,3072]{4,3,2,1,0:T(8,128)(2,1)S(1)}, u32[]{:S(2)}, u32[]{:S(2)}) %collective-permute-start.3) | collective-permute-done | bytes 393248 | tf_op jit(solution)/shard_map/ppermute | solution.py:103
  21.7 2.9 collective-permute-start.4
  52.0 3.7 collective-permute-done.21
  58.9 8.5 %collective-permute-done.17 = bf16[2,2,1,1,64,768]{5,4,3,2,1,0:T(8,128)(2,1)S(1)} collective-permute-done((bf16[2,2,1,1,64,768]{5,4,3,2,1,0:T(8,128)(2,1)S(1)}, bf16[2,2,1,1,64,768]{5,4,3,2,1,0:T(8,128)(2,1)S(1)}, u32[]{:S(2)}, u32[]{:S(2)}) %collective-permute-start.17) | collective-permute-done | bytes 393248 | tf_op jit(solution)/shard_map/ppermute | solution.py:58
  73.8 4.2 collective-permute-done.29
  83.4 13.0 %collective-permute-done.25 = bf16[2,2,2,1,64,768]{5,4,3,2,1,0:T(8,128)(2,1)S(1)} collective-permute-done((bf16[2,2,2,1,64,768]{5,4,3,2,1,0:T(8,128)(2,1)S(1)}, bf16[2,2,2,1,64,768]{5,4,3,2,1,0:T(8,128)(2,1)S(1)}, u32[]{:S(2)}, u32[]{:S(2)}) %collective-permute-start.25) | collective-permute-done | bytes 786464 | tf_op jit(solution)/shard_map/ppermute | solution.py:58
  103.8 19.9 %collective-permute-start.37 = (bf16[256,1024]{1,0:T(8,128)(2,1)S(1)}, bf16[256,1024]{1,0:T(8,128)(2,1)S(1)}, u32[]{:S(2)}, u32[]{:S(2)}) collective-permute-start(bf16[256,1024]{1,0:T(8,128)(2,1)S(1)} %multiply_convert_fusion.2), channel_id=1, source_target_pairs={{0,4},{4,0},{1,5},{5,1},{2,6},{6,2},{3,7},{7,3},{8,12},{12,8},{9,1... | collective-permute-start | bytes 1572872 | tf_op jit(solution)/shard_map/ppermute | solution.py:47
  125.6 2.8 shard_map.171
  129.2 2.8 shard_map.172
  133.0 2.8 shard_map.173
  135.8 2.8 shard_map.174
  150.8 16.6 %shard_map.175 = (bf16[512,1536]{1,0:T(8,128)(2,1)S(1)}, bf16[512,3072]{1,0:T(8,128)(2,1)}, f32[512,1024]{1,0:T(8,128)S(1)}, f32[512,1024]{1,0:T(8,128)}) custom-call(bf16[512,1024]{1,0:T(8,128)(2,1)S(1)} %pad_maximum_fusion.13.input_ref.first_left, bf16[512,1024]{1,0:T(8,128)(2,1)S(1)} %pad_maximum_fusion.14.grad_ref.second_left, ...), custom_call_target="tpu_custom_call" | custom-call | flops 1048576 | bytes 65536 | tf_op jit(solution)/shard_map/pallas_call | solution.py:445
  180.3 3.7 shard_map.178
  184.5 3.7 shard_map.177
  192.0 5.2 %shard_map.176 = (bf16[512,512]{1,0:T(8,128)(2,1)S(1)}, f32[16,128]{1,0:T(8,128)S(1)}, f32[512,1024]{1,0:T(8,128)S(1)}) custom-call(f32[512,512]{1,0:T(8,128)S(1)} %copy-done.10, bf16[512,1024]{1,0:T(8,128)(2,1)S(1)} %pad_maximum_fusion.15.branch_ref.second_left, bf16[1024,768]{1,0:T(8,128)(2,1)S(1)} %bitcast.144, ...), custom_call_target="tpu_custom_call" | custom-call | flops 1048576 | bytes 65536 | tf_op jit(solution)/shard_map/pallas_call | solution.py:391
  197.2 5.2 %shard_map.181 = (bf16[512,512]{1,0:T(8,128)(2,1)S(1)}, f32[16,128]{1,0:T(8,128)S(1)}, f32[512,1024]{1,0:T(8,128)S(1)}) custom-call(f32[512,512]{1,0:T(8,128)S(1)} %copy-done.8, bf16[512,1024]{1,0:T(8,128)(2,1)S(1)} %pad_maximum_fusion.15.branch_ref.second_left, bf16[1024,768]{1,0:T(8,128)(2,1)S(1)} %bitcast.142, f32[512,128]{1,0:T(8,128)S(1)} %get-tuple-element.627.cos_ref, ...), custom_call_target="tpu_custom_call" | custom-call | flops 1048576 | bytes 65536 | tf_op jit(solution)/shard_map/pallas_call | solution.py:391
  203.3 3.9 collective-permute-done.47
  207.2 4.3 collective-permute-done.46
  211.4 3.4 collective-permute-done.45
  223.6 5.2 %shard_map.183 = (bf16[512,512]{1,0:T(8,128)(2,1)S(1)}, f32[16,128]{1,0:T(8,128)S(1)}, f32[512,1024]{1,0:T(8,128)S(1)}) custom-call(f32[512,512]{1,0:T(8,128)S(1)} %copy-done.6, bf16[512,1024]{1,0:T(8,128)(2,1)S(1)} %pad_maximum_fusion.15.branch_ref.second_left, bf16[1024,768]{1,0:T(8,128)(2,1)S(1)} %bitcast.140, f32[512,128]{1,0:T(8,128)S(1)} %get-tuple-element.627.cos_ref, ...), custom_call_target="tpu_custom_call" | custom-call | flops 1048576 | bytes 65536 | tf_op jit(solution)/shard_map/pallas_call | solution.py:391
  239.6 5.2 %shard_map.185 = (bf16[512,512]{1,0:T(8,128)(2,1)S(1)}, f32[16,128]{1,0:T(8,128)S(1)}, f32[512,1024]{1,0:T(8,128)S(1)}) custom-call(f32[512,512]{1,0:T(8,128)S(1)} %get-tuple-element.389.raw_ref, bf16[512,1024]{1,0:T(8,128)(2,1)S(1)} %pad_maximum_fusion.15.branch_ref.second_left, bf16[1024,768]{1,0:T(8,128)(2,1)S(1)} %bitcast.138, ...), custom_call_target="tpu_custom_call" | custom-call | flops 1048576 | bytes 65536 | tf_op jit(solution)/shard_map/pallas_call | solution.py:391
  255.1 5.2 %collective-permute-start.61 = (bf16[256,1024]{1,0:T(8,128)(2,1)S(1)}, bf16[256,1024]{1,0:T(8,128)(2,1)S(1)}, u32[]{:S(2)}, u32[]{:S(2)}) collective-permute-start(bf16[256,1024]{1,0:T(8,128)(2,1)S(1)} %slice.832), channel_id=1, source_target_pairs={{0,4},{4,0},{1,5},{5,1},{2,6},{6,2},{3,7},{7,3},{8,12},{12,8},{9,1... | collective-permute-start | bytes 1572872 | tf_op jit(solution)/shard_map/ppermute | solution.py:47
  268.7 10.9 %collective-permute-done.58 = bf16[2,1,2,2,64,768]{5,4,3,2,1,0:T(8,128)(2,1)S(1)} collective-permute-done((bf16[2,1,2,2,64,768]{5,4,3,2,1,0:T(8,128)(2,1)S(1)}, bf16[2,1,2,2,64,768]{5,4,3,2,1,0:T(8,128)(2,1)S(1)}, u32[]{:S(2)}, u32[]{:S(2)}) %collective-permute-start.58) | collective-permute-done | bytes 786464 | tf_op jit(solution)/shard_map/ppermute | solution.py:83
  287.0 3.3 collective-permute-done.62
  314.0 6.8 %collective-permute-start.81 = (bf16[32,7680]{1,0:T(8,128)(2,1)S(1)}, bf16[32,7680]{1,0:T(8,128)(2,1)S(1)}, u32[]{:S(2)}, u32[]{:S(2)}) collective-permute-start(bf16[32,7680]{1,0:T(8,128)(2,1)S(1)} %get-tuple-element.549), channel_id=1, source_target_pairs={{0,4},{4,0},{1,5},{5,1},{2,6},{6,2},{3,7},{7,3},{8,12},{12,8},{9,1... | collective-permute-start | bytes 1474568 | tf_op jit(solution)/shard_map/ppermute | solution.py:47
  325.9 7.7 %collective-permute-done.82 = bf16[4,16,3072]{2,1,0:T(8,128)(2,1)S(1)} collective-permute-done((bf16[4,16,3072]{2,1,0:T(8,128)(2,1)S(1)}, bf16[4,16,3072]{2,1,0:T(8,128)(2,1)S(1)}, u32[]{:S(2)}, u32[]{:S(2)}) %collective-permute-start.82) | collective-permute-done | bytes 393248 | tf_op jit(solution)/shard_map/ppermute | solution.py:778
  337.4 4.2 collective-permute-done.84
  357.9 2.9 collective-permute-done.92
  365.7 4.8 %collective-permute-start.42 = (bf16[256,1024]{1,0:T(8,128)(2,1)S(1)}, bf16[256,1024]{1,0:T(8,128)(2,1)S(1)}, u32[]{:S(2)}, u32[]{:S(2)}) collective-permute-start(bf16[256,1024]{1,0:T(8,128)(2,1)S(1)} %slice.834), channel_id=1, source_target_pairs={{0,4},{4,0},{1,5},{5,1},{2,6},{6,2},{3,7},{7,3},{8,12},{12,8},{9,1... | collective-permute-start | bytes 1572872 | tf_op jit(solution)/shard_map/ppermute | solution.py:47
  379.6 9.1 %collective-permute-done.100.refs_3_ = bf16[1,2,2,2,64,768]{5,4,3,2,1,0:T(8,128)(2,1)S(1)} collective-permute-done((bf16[1,2,2,2,64,768]{5,4,3,2,1,0:T(8,128)(2,1)S(1)}, bf16[1,2,2,2,64,768]{5,4,3,2,1,0:T(8,128)(2,1)S(1)}, u32[]{:S(2)}, u32[]{:S(2)}) %collective-permute-start.100) | collective-permute-done | bytes 786464 | tf_op jit(solution)/shard_map/ppermute | solution.py:58
  405.2 46.5 %shard_map.189 = bf16[64,3072]{1,0:T(8,128)(2,1)S(1)} custom-call(bf16[2,2,2,1,64,896]{5,4,3,2,1,0:T(8,128)(2,1)S(1)} %pad_maximum_fusion.16.refs_0_, bf16[2,2,2,1,64,896]{5,4,3,2,1,0:T(8,128)(2,1)} %copy-done.38, bf16[1,2,2,2,64,768]{5,4,3,2,1,0:T(8,128)(2,1)S(1)} %copy-done.12, bf16[1,2,2,2,64,768]{5,4,3,2,1,0:T(8,128)(2,1)S(1)} %copy-done.22, ...), custom_call_target="tpu_custom_call" | custom-call | flops 49999998976 | bytes 8388608 | tf_op jit(solution)/shard_map/pallas_call | solution.py:336
  451.7 6.4 %collective-permute-start.103 = (bf16[32,3072]{1,0:T(8,128)(2,1)S(1)}, bf16[32,3072]{1,0:T(8,128)(2,1)S(1)}, u32[]{:S(2)}, u32[]{:S(2)}) collective-permute-start(bf16[32,3072]{1,0:T(8,128)(2,1)S(1)} %broadcast_select_fusion.2), channel_id=1, source_target_pairs={{0,4},{4,0},{1,5},{5,1},{2,6},{6,2},{3,7},{7,3},{8,12},{12,8},{9,1... | collective-permute-start | bytes 589832 | tf_op jit(solution)/shard_map/ppermute | solution.py:47
  (480 shorter events, 221.0 us)
Async XLA Ops:
  5.9 97.9 %collective-permute-start.38 = (s32[2,128]{1,0:T(2,128)}, s32[2,128]{1,0:T(2,128)S(1)}, u32[]{:S(2)}, u32[]{:S(2)}) collective-permute-start(s32[2,128]{1,0:T(2,128)} %param.14), channel_id=1, source_target_pairs={{0,4},{4,0},{1,5},{5,1},{2,6},{6,2},{3,7},{7,3},{8,12},{12,8},{9,1... | collective-permute-start | bytes 3080 | tf_op jit(solution)/shard_map/ppermute | solution.py:47
  78.1 18.3 %collective-permute-start.25 = (bf16[2,2,2,1,64,768]{5,4,3,2,1,0:T(8,128)(2,1)S(1)}, bf16[2,2,2,1,64,768]{5,4,3,2,1,0:T(8,128)(2,1)S(1)}, u32[]{:S(2)}, u32[]{:S(2)}) collective-permute-start(bf16[2,2,2,1,64,768]{5,4,3,2,1,0:T(8,128)(2,1)S(1)} %pad_maximum_fusion.19), channel_id=1, source_target_pairs={{0,24},{24,0},{8,16},{16,8},{1,25},{25,1},{9,17},{17,9},{2,26},{26... | collective-permute-start | bytes 2359304 | tf_op jit(solution)/shard_map/ppermute | solution.py:58
  80.5 16.2 %collective-permute-start.26 = (bf16[1,2,2,2,64,768]{5,4,3,2,1,0:T(8,128)(2,1)S(1)}, bf16[1,2,2,2,64,768]{5,4,3,2,1,0:T(8,128)(2,1)S(1)}, u32[]{:S(2)}, u32[]{:S(2)}) collective-permute-start(bf16[1,2,2,2,64,768]{5,4,3,2,1,0:T(8,128)(2,1)S(1)} %pad_maximum_fusion.20), channel_id=1, source_target_pairs={{0,32},{32,0},{64,96},{96,64},{1,33},{33,1},{65,97},{97,65},{2,34}... | collective-permute-start | bytes 2359304 | tf_op jit(solution)/shard_map/ppermute | solution.py:58
  81.1 17.1 %collective-permute-start.27 = (bf16[2,1,2,2,64,768]{5,4,3,2,1,0:T(8,128)(2,1)S(1)}, bf16[2,1,2,2,64,768]{5,4,3,2,1,0:T(8,128)(2,1)S(1)}, u32[]{:S(2)}, u32[]{:S(2)}) collective-permute-start(bf16[2,1,2,2,64,768]{5,4,3,2,1,0:T(8,128)(2,1)S(1)} %pad_maximum_fusion.21), channel_id=1, source_target_pairs={{0,8},{8,0},{16,24},{24,16},{1,9},{9,1},{17,25},{25,17},{2,10},{10... | collective-permute-start | bytes 2359304 | tf_op jit(solution)/shard_map/ppermute | solution.py:58
  82.1 16.0 %collective-permute-start.28 = (bf16[2,2,1,2,64,768]{5,4,3,2,1,0:T(8,128)(2,1)S(1)}, bf16[2,2,1,2,64,768]{5,4,3,2,1,0:T(8,128)(2,1)S(1)}, u32[]{:S(2)}, u32[]{:S(2)}) collective-permute-start(bf16[2,2,1,2,64,768]{5,4,3,2,1,0:T(8,128)(2,1)S(1)} %pad_maximum_fusion.22), channel_id=1, source_target_pairs={{0,96},{96,0},{32,64},{64,32},{1,97},{97,1},{33,65},{65,33},{2,98}... | collective-permute-start | bytes 2359304 | tf_op jit(solution)/shard_map/ppermute | solution.py:58
  98.8 39.9 %collective-permute-start.33 = (bf16[2,2,2,1,64,1152]{5,4,3,2,1,0:T(8,128)(2,1)S(1)}, bf16[2,2,2,1,64,1152]{5,4,3,2,1,0:T(8,128)(2,1)S(1)}, u32[]{:S(2)}, u32[]{:S(2)}) collective-permute-start(bf16[2,2,2,1,64,1152]{5,4,3,2,1,0:T(8,128)(2,1)S(1)} %pad_maximum_fusion.8), channel_id=1, source_target_pairs={{0,24},{24,0},{8,16},{16,8},{1,25},{25,1},{9,17},{17,9},{2,26},{26... | collective-permute-start | bytes 3538952 | tf_op jit(solution)/shard_map/ppermute | solution.py:58
  101.1 37.7 %collective-permute-start.34 = (bf16[1,2,2,2,64,1152]{5,4,3,2,1,0:T(8,128)(2,1)S(1)}, bf16[1,2,2,2,64,1152]{5,4,3,2,1,0:T(8,128)(2,1)S(1)}, u32[]{:S(2)}, u32[]{:S(2)}) collective-permute-start(bf16[1,2,2,2,64,1152]{5,4,3,2,1,0:T(8,128)(2,1)S(1)} %pad_maximum_fusion.9), channel_id=1, source_target_pairs={{0,32},{32,0},{64,96},{96,64},{1,33},{33,1},{65,97},{97,65},{2,34}... | collective-permute-start | bytes 3538952 | tf_op jit(solution)/shard_map/ppermute | solution.py:58
  101.7 37.0 %collective-permute-start.35 = (bf16[2,1,2,2,64,1152]{5,4,3,2,1,0:T(8,128)(2,1)S(1)}, bf16[2,1,2,2,64,1152]{5,4,3,2,1,0:T(8,128)(2,1)S(1)}, u32[]{:S(2)}, u32[]{:S(2)}) collective-permute-start(bf16[2,1,2,2,64,1152]{5,4,3,2,1,0:T(8,128)(2,1)S(1)} %pad_maximum_fusion.10), channel_id=1, source_target_pairs={{0,8},{8,0},{16,24},{24,16},{1,9},{9,1},{17,25},{25,17},{2,10},{10... | collective-permute-start | bytes 3538952 | tf_op jit(solution)/shard_map/ppermute | solution.py:58
  101.7 37.0 %collective-permute-start.36 = (bf16[2,2,1,2,64,1152]{5,4,3,2,1,0:T(8,128)(2,1)S(1)}, bf16[2,2,1,2,64,1152]{5,4,3,2,1,0:T(8,128)(2,1)S(1)}, u32[]{:S(2)}, u32[]{:S(2)}) collective-permute-start(bf16[2,2,1,2,64,1152]{5,4,3,2,1,0:T(8,128)(2,1)S(1)} %pad_maximum_fusion.11), channel_id=1, source_target_pairs={{0,96},{96,0},{32,64},{64,32},{1,97},{97,1},{33,65},{65,33},{2,98}... | collective-permute-start | bytes 3538952 | tf_op jit(solution)/shard_map/ppermute | solution.py:58
  103.8 21.5 %collective-permute-start.37 = (bf16[256,1024]{1,0:T(8,128)(2,1)S(1)}, bf16[256,1024]{1,0:T(8,128)(2,1)S(1)}, u32[]{:S(2)}, u32[]{:S(2)}) collective-permute-start(bf16[256,1024]{1,0:T(8,128)(2,1)S(1)} %multiply_convert_fusion.2), channel_id=1, source_target_pairs={{0,4},{4,0},{1,5},{5,1},{2,6},{6,2},{3,7},{7,3},{8,12},{12,8},{9,1... | collective-permute-start | bytes 1572872 | tf_op jit(solution)/shard_map/ppermute | solution.py:47
  169.4 18.8 %collective-permute-start.43 = (bf16[256,1024]{1,0:T(8,128)(2,1)S(1)}, bf16[256,1024]{1,0:T(8,128)(2,1)S(1)}, u32[]{:S(2)}, u32[]{:S(2)}) collective-permute-start(bf16[256,1024]{1,0:T(8,128)(2,1)S(1)} %slice.833), channel_id=1, source_target_pairs={{0,4},{4,0},{1,5},{5,1},{2,6},{6,2},{3,7},{7,3},{8,12},{12,8},{9,1... | collective-permute-start | bytes 1572872 | tf_op jit(solution)/shard_map/ppermute | solution.py:47
  174.4 28.8 %collective-permute-start.48 = (bf16[2,2,2,1,64,1152]{5,4,3,2,1,0:T(8,128)(2,1)S(1)}, bf16[2,2,2,1,64,1152]{5,4,3,2,1,0:T(8,128)(2,1)}, u32[]{:S(2)}, u32[]{:S(2)}) collective-permute-start(bf16[2,2,2,1,64,1152]{5,4,3,2,1,0:T(8,128)(2,1)S(1)} %bitcast.153), channel_id=1, source_target_pairs={{0,24},{24,0},{8,16},{16,8},{1,25},{25,1},{9,17},{17,9},{2,26},{26... | collective-permute-start | bytes 3538952 | tf_op jit(solution)/shard_map/ppermute | solution.py:83
  178.7 28.5 %collective-permute-start.47 = (bf16[2,2,1,2,64,1152]{5,4,3,2,1,0:T(8,128)(2,1)S(1)}, bf16[2,2,1,2,64,1152]{5,4,3,2,1,0:T(8,128)(2,1)}, u32[]{:S(2)}, u32[]{:S(2)}) collective-permute-start(bf16[2,2,1,2,64,1152]{5,4,3,2,1,0:T(8,128)(2,1)S(1)} %bitcast.154), channel_id=1, source_target_pairs={{0,96},{96,0},{32,64},{64,32},{1,97},{97,1},{33,65},{65,33},{2,98}... | collective-permute-start | bytes 3538952 | tf_op jit(solution)/shard_map/ppermute | solution.py:83
  184.0 27.5 %collective-permute-start.46 = (bf16[2,1,2,2,64,1152]{5,4,3,2,1,0:T(8,128)(2,1)}, bf16[2,1,2,2,64,1152]{5,4,3,2,1,0:T(8,128)(2,1)}, u32[]{:S(2)}, u32[]{:S(2)}) collective-permute-start(bf16[2,1,2,2,64,1152]{5,4,3,2,1,0:T(8,128)(2,1)} %bitcast.33), channel_id=1, source_target_pairs={{0,8},{8,0},{16,24},{24,16},{1,9},{9,1},{17,25},{25,17},{2,10},{10... | collective-permute-start | bytes 3538952 | tf_op jit(solution)/shard_map/ppermute | solution.py:83
  188.2 26.7 %collective-permute-start.45 = (bf16[1,2,2,2,64,1152]{5,4,3,2,1,0:T(8,128)(2,1)}, bf16[1,2,2,2,64,1152]{5,4,3,2,1,0:T(8,128)(2,1)S(1)}, u32[]{:S(2)}, u32[]{:S(2)}) collective-permute-start(bf16[1,2,2,2,64,1152]{5,4,3,2,1,0:T(8,128)(2,1)} %bitcast.32), channel_id=1, source_target_pairs={{0,32},{32,0},{64,96},{96,64},{1,33},{33,1},{65,97},{97,65},{2,34}... | collective-permute-start | bytes 3538952 | tf_op jit(solution)/shard_map/ppermute | solution.py:83
  219.8 13.0 %collective-permute-start.49 = (bf16[1,1,2,2,64,1152]{5,4,3,2,1,0:T(8,128)(2,1)S(1)}, bf16[1,1,2,2,64,1152]{5,4,3,2,1,0:T(8,128)(2,1)S(1)}, u32[]{:S(2)}, u32[]{:S(2)}) collective-permute-start(bf16[1,1,2,2,64,1152]{5,4,3,2,1,0:T(8,128)(2,1)S(1)} %get-tuple-element.357), channel_id=1, source_target_pairs={{0,8},{8,0},{16,24},{24,16},{1,9},{9,1},{17,25},{25,17},{2,10},{10... | collective-permute-start | bytes 1769480 | tf_op jit(solution)/shard_map/ppermute | solution.py:83
  221.2 13.8 %collective-permute-start.50 = (bf16[2,1,1,2,64,1152]{5,4,3,2,1,0:T(8,128)(2,1)S(1)}, bf16[2,1,1,2,64,1152]{5,4,3,2,1,0:T(8,128)(2,1)S(1)}, u32[]{:S(2)}, u32[]{:S(2)}) collective-permute-start(bf16[2,1,1,2,64,1152]{5,4,3,2,1,0:T(8,128)(2,1)S(1)} %get-tuple-element.358), channel_id=1, source_target_pairs={{0,96},{96,0},{32,64},{64,32},{1,97},{97,1},{33,65},{65,33},{2,98}... | collective-permute-start | bytes 1769480 | tf_op jit(solution)/shard_map/ppermute | solution.py:83
  222.4 13.5 %collective-permute-start.51 = (bf16[2,2,1,1,64,1152]{5,4,3,2,1,0:T(8,128)(2,1)S(1)}, bf16[2,2,1,1,64,1152]{5,4,3,2,1,0:T(8,128)(2,1)S(1)}, u32[]{:S(2)}, u32[]{:S(2)}) collective-permute-start(bf16[2,2,1,1,64,1152]{5,4,3,2,1,0:T(8,128)(2,1)S(1)} %get-tuple-element.359), channel_id=1, source_target_pairs={{0,24},{24,0},{8,16},{16,8},{1,25},{25,1},{9,17},{17,9},{2,26},{26... | collective-permute-start | bytes 1769480 | tf_op jit(solution)/shard_map/ppermute | solution.py:83
  223.6 12.3 %collective-permute-start.52 = (bf16[1,2,2,1,64,1152]{5,4,3,2,1,0:T(8,128)(2,1)S(1)}, bf16[1,2,2,1,64,1152]{5,4,3,2,1,0:T(8,128)(2,1)S(1)}, u32[]{:S(2)}, u32[]{:S(2)}) collective-permute-start(bf16[1,2,2,1,64,1152]{5,4,3,2,1,0:T(8,128)(2,1)S(1)} %get-tuple-element.360), channel_id=1, source_target_pairs={{0,32},{32,0},{64,96},{96,64},{1,33},{33,1},{65,97},{97,65},{2,34}... | collective-permute-start | bytes 1769480 | tf_op jit(solution)/shard_map/ppermute | solution.py:83
  236.6 16.0 %collective-permute-start.54 = (bf16[1,1,1,2,64,1152]{5,4,3,2,1,0:T(8,128)(2,1)S(1)}, bf16[1,1,1,2,64,1152]{5,4,3,2,1,0:T(8,128)(2,1)S(1)}, u32[]{:S(2)}, u32[]{:S(2)}) collective-permute-start(bf16[1,1,1,2,64,1152]{5,4,3,2,1,0:T(8,128)(2,1)S(1)} %get-tuple-element.374), channel_id=1, source_target_pairs={{0,96},{96,0},{32,64},{64,32},{1,97},{97,1},{33,65},{65,33},{2,98}... | collective-permute-start | bytes 884744 | tf_op jit(solution)/shard_map/ppermute | solution.py:83
  238.2 15.7 %collective-permute-start.55 = (bf16[2,1,1,1,64,1152]{5,4,3,2,1,0:T(8,128)(2,1)S(1)}, bf16[2,1,1,1,64,1152]{5,4,3,2,1,0:T(8,128)(2,1)S(1)}, u32[]{:S(2)}, u32[]{:S(2)}) collective-permute-start(bf16[2,1,1,1,64,1152]{5,4,3,2,1,0:T(8,128)(2,1)S(1)} %get-tuple-element.375), channel_id=1, source_target_pairs={{0,24},{24,0},{8,16},{16,8},{1,25},{25,1},{9,17},{17,9},{2,26},{26... | collective-permute-start | bytes 884744 | tf_op jit(solution)/shard_map/ppermute | solution.py:83
  239.4 15.3 %collective-permute-start.56 = (bf16[1,2,1,1,64,1152]{5,4,3,2,1,0:T(8,128)(2,1)S(1)}, bf16[1,2,1,1,64,1152]{5,4,3,2,1,0:T(8,128)(2,1)S(1)}, u32[]{:S(2)}, u32[]{:S(2)}) collective-permute-start(bf16[1,2,1,1,64,1152]{5,4,3,2,1,0:T(8,128)(2,1)S(1)} %get-tuple-element.376), channel_id=1, source_target_pairs={{0,32},{32,0},{64,96},{96,64},{1,33},{33,1},{65,97},{97,65},{2,34}... | collective-permute-start | bytes 884744 | tf_op jit(solution)/shard_map/ppermute | solution.py:83
  239.4 15.3 %collective-permute-start.57 = (bf16[1,1,2,1,64,1152]{5,4,3,2,1,0:T(8,128)(2,1)S(1)}, bf16[1,1,2,1,64,1152]{5,4,3,2,1,0:T(8,128)(2,1)S(1)}, u32[]{:S(2)}, u32[]{:S(2)}) collective-permute-start(bf16[1,1,2,1,64,1152]{5,4,3,2,1,0:T(8,128)(2,1)S(1)} %get-tuple-element.377), channel_id=1, source_target_pairs={{0,8},{8,0},{16,24},{24,16},{1,9},{9,1},{17,25},{25,17},{2,10},{10... | collective-permute-start | bytes 884744 | tf_op jit(solution)/shard_map/ppermute | solution.py:83
  246.9 21.7 %collective-permute-start.60 = (bf16[2,2,2,1,64,768]{5,4,3,2,1,0:T(8,128)(2,1)S(1)}, bf16[2,2,2,1,64,768]{5,4,3,2,1,0:T(8,128)(2,1)S(1)}, u32[]{:S(2)}, u32[]{:S(2)}) collective-permute-start(bf16[2,2,2,1,64,768]{5,4,3,2,1,0:T(8,128)(2,1)S(1)} %bitcast.157), channel_id=1, source_target_pairs={{0,24},{24,0},{8,16},{16,8},{1,25},{25,1},{9,17},{17,9},{2,26},{26... | collective-permute-start | bytes 2359304 | tf_op jit(solution)/shard_map/ppermute | solution.py:83
  252.6 16.1 %collective-permute-start.59 = (bf16[2,2,1,2,64,768]{5,4,3,2,1,0:T(8,128)(2,1)S(1)}, bf16[2,2,1,2,64,768]{5,4,3,2,1,0:T(8,128)(2,1)S(1)}, u32[]{:S(2)}, u32[]{:S(2)}) collective-permute-start(bf16[2,2,1,2,64,768]{5,4,3,2,1,0:T(8,128)(2,1)S(1)} %bitcast.158), channel_id=1, source_target_pairs={{0,96},{96,0},{32,64},{64,32},{1,97},{97,1},{33,65},{65,33},{2,98}... | collective-permute-start | bytes 2359304 | tf_op jit(solution)/shard_map/ppermute | solution.py:83
  253.9 14.9 %collective-permute-start.53 = (bf16[1,2,2,2,64,768]{5,4,3,2,1,0:T(8,128)(2,1)S(1)}, bf16[1,2,2,2,64,768]{5,4,3,2,1,0:T(8,128)(2,1)S(1)}, u32[]{:S(2)}, u32[]{:S(2)}) collective-permute-start(bf16[1,2,2,2,64,768]{5,4,3,2,1,0:T(8,128)(2,1)S(1)} %bitcast.155), channel_id=1, source_target_pairs={{0,32},{32,0},{64,96},{96,64},{1,33},{33,1},{65,97},{97,65},{2,34}... | collective-permute-start | bytes 2359304 | tf_op jit(solution)/shard_map/ppermute | solution.py:83
  260.4 19.2 %collective-permute-start.58 = (bf16[2,1,2,2,64,768]{5,4,3,2,1,0:T(8,128)(2,1)S(1)}, bf16[2,1,2,2,64,768]{5,4,3,2,1,0:T(8,128)(2,1)S(1)}, u32[]{:S(2)}, u32[]{:S(2)}) collective-permute-start(bf16[2,1,2,2,64,768]{5,4,3,2,1,0:T(8,128)(2,1)S(1)} %bitcast.156), channel_id=1, source_target_pairs={{0,8},{8,0},{16,24},{24,16},{1,9},{9,1},{17,25},{25,17},{2,10},{10... | collective-permute-start | bytes 2359304 | tf_op jit(solution)/shard_map/ppermute | solution.py:83
  365.7 11.8 %collective-permute-start.42 = (bf16[256,1024]{1,0:T(8,128)(2,1)S(1)}, bf16[256,1024]{1,0:T(8,128)(2,1)S(1)}, u32[]{:S(2)}, u32[]{:S(2)}) collective-permute-start(bf16[256,1024]{1,0:T(8,128)(2,1)S(1)} %slice.834), channel_id=1, source_target_pairs={{0,4},{4,0},{1,5},{5,1},{2,6},{6,2},{3,7},{7,3},{8,12},{12,8},{9,1... | collective-permute-start | bytes 1572872 | tf_op jit(solution)/shard_map/ppermute | solution.py:47
  373.3 18.6 %collective-permute-start.99 = (bf16[2,2,2,1,64,896]{5,4,3,2,1,0:T(8,128)(2,1)S(1)}, bf16[2,2,2,1,64,896]{5,4,3,2,1,0:T(8,128)(2,1)S(1)}, u32[]{:S(2)}, u32[]{:S(2)}) collective-permute-start(bf16[2,2,2,1,64,896]{5,4,3,2,1,0:T(8,128)(2,1)S(1)} %pad_maximum_fusion.16.refs_0_), channel_id=1, source_target_pairs={{0,24},{24,0},{8,16},{16,8},{1,25},{25,1},{9,17},{17,9},{2,26},{26... | collective-permute-start | bytes 2752520 | tf_op jit(solution)/shard_map/ppermute | solution.py:58
  374.6 14.1 %collective-permute-start.100 = (bf16[1,2,2,2,64,768]{5,4,3,2,1,0:T(8,128)(2,1)S(1)}, bf16[1,2,2,2,64,768]{5,4,3,2,1,0:T(8,128)(2,1)S(1)}, u32[]{:S(2)}, u32[]{:S(2)}) collective-permute-start(bf16[1,2,2,2,64,768]{5,4,3,2,1,0:T(8,128)(2,1)S(1)} %pad_maximum_fusion.24.refs_2_), channel_id=1, source_target_pairs={{0,32},{32,0},{64,96},{96,64},{1,33},{33,1},{65,97},{97,65},{2,34}... | collective-permute-start | bytes 2359304 | tf_op jit(solution)/shard_map/ppermute | solution.py:58
  375.7 13.8 %collective-permute-start.101 = (bf16[2,1,2,2,64,768]{5,4,3,2,1,0:T(8,128)(2,1)S(1)}, bf16[2,1,2,2,64,768]{5,4,3,2,1,0:T(8,128)(2,1)S(1)}, u32[]{:S(2)}, u32[]{:S(2)}) collective-permute-start(bf16[2,1,2,2,64,768]{5,4,3,2,1,0:T(8,128)(2,1)S(1)} %pad_maximum_fusion.25.refs_4_), channel_id=1, source_target_pairs={{0,8},{8,0},{16,24},{24,16},{1,9},{9,1},{17,25},{25,17},{2,10},{10... | collective-permute-start | bytes 2359304 | tf_op jit(solution)/shard_map/ppermute | solution.py:58
  375.7 14.7 %collective-permute-start.102 = (bf16[2,2,1,2,64,768]{5,4,3,2,1,0:T(8,128)(2,1)S(1)}, bf16[2,2,1,2,64,768]{5,4,3,2,1,0:T(8,128)(2,1)S(1)}, u32[]{:S(2)}, u32[]{:S(2)}) collective-permute-start(bf16[2,2,1,2,64,768]{5,4,3,2,1,0:T(8,128)(2,1)S(1)} %pad_maximum_fusion.26.refs_6_), channel_id=1, source_target_pairs={{0,96},{96,0},{32,64},{64,32},{1,97},{97,1},{33,65},{65,33},{2,98}... | collective-permute-start | bytes 2359304 | tf_op jit(solution)/shard_map/ppermute | solution.py:58
  (119 other events, 1256.2 us)
where the time goes:
time: 470 us; the launch traced here: 461 us
  starting transfers between devices  142 us (30%)
  waiting for transfers between devices  134 us (29%)
  Pallas kernels  118 us (25%)
  other arithmetic  32 us (7%)
  local copies, waits for them, and re-layouts  16 us (3%)
  matrix products  14.1 us (3%)
  between operations  5.22 us (1%)
    ppermute x48, waiting for transfers between devices, gather_came(): fresh.append(lax.ppermute(quarters[i], axis, pairs))  58.8 us
    ppermute x14, starting transfers between devices, swap(): return lax.ppermute(x, 'dp_2', ((0, 1), (1, 0)))  54.7 us
    pallas_call x1, Pallas kernels, iterate_rows(): pl.pallas_call(iterate_kernel, in_specs=[pl.BlockSpec(memory_space=pl.ANY...  46.5 us
    ppermute x48, starting transfers between devices, gather_came(): fresh.append(lax.ppermute(quarters[i], axis, pairs))  46.2 us
    ppermute x32, waiting for transfers between devices, scatter_step(): came.append(lax.ppermute(sent[i], axis, pairs))  43 us
    ppermute x32, starting transfers between devices, scatter_step(): came.append(lax.ppermute(sent[i], axis, pairs))  28.3 us
    pallas_call x8, Pallas kernels, terms(): pl.pallas_call(functools.partial(terms_kernel, link), grid=(4,), in_specs...  21 us
    pallas_call x4, Pallas kernels, heads_backward(): pl.pallas_call(heads_back_kernel, grid=(tokens // (2 * SEQ),), in_specs=[...  20.8 us
  transfers between devices with their start and end apart: 104, of which 58 were waited for; matrix products, arithmetic and copies ran while one was open for 5% of the time, Pallas kernels for 12%

commit v1 on v0

--- a/solution.py
+++ b/solution.py
@@ -125,6 +125,17 @@
     return jnp.concatenate([u[:, HD // 2 :], u[:, : HD // 2]], axis=1)
 
 
+def fetch(pieces, quarter, arrived, link):
+    copies = []
+    for part in range(2):
+        place = [slice(None)] * 4
+        place[link] = slice(part, part + 1)
+        copies.append(
+            pltpu.make_async_copy(pieces[part], quarter.at[tuple(place)], arrived.at[part])
+        )
+    return copies
+
+
 def head_forward(raw, gain, cosine, sine):
     scale = lax.rsqrt(jnp.mean(raw * raw, axis=-1, keepdims=True) + norm_eps)
     normed = raw * scale
@@ -151,8 +162,29 @@
 
 
 def heads_kernel(
-    input_ref, weight_ref, cos_ref, sin_ref, gain_ref, sum_ref, raw_ref, attn_ref, out_ref
+    link,
+    input_ref,
+    held_ref,
+    fresh_ref,
+    cos_ref,
+    sin_ref,
+    gain_ref,
+    sum_ref,
+    raw_ref,
+    attn_ref,
+    out_ref,
+    quarter,
+    arrived,
 ):
+    @pl.when(pl.program_id(0) == 0)
+    def _():
+        copies = fetch((held_ref, fresh_ref), quarter, arrived, link)
+        for copy in copies:
+            copy.start()
+        for copy in copies:
+            copy.wait()
+
+    weight_ref = quarter.reshape(D, HEADS_WIDTH)
     raw_ref[...] = dot(input_ref[...], weight_ref[:, : 4 * HD])
     for b in range(raw_ref.shape[0] // SEQ):
         at = slice(b * SEQ, (b + 1) * SEQ)
@@ -178,9 +210,11 @@
 
 
 def heads_back_kernel(
+    link,
     raw_ref,
     branch_ref,
-    weight_ref,
+    held_ref,
+    fresh_ref,
     cos_ref,
     sin_ref,
     gain_ref,
@@ -189,7 +223,18 @@
     term_ref,
     one_ref,
     grad_ref,
+    quarter,
+    arrived,
 ):
+    @pl.when(pl.program_id(0) == 0)
+    def _():
+        copies = fetch((held_ref, fresh_ref), quarter, arrived, link)
+        for copy in copies:
+            copy.start()
+        for copy in copies:
+            copy.wait()
+
+    weight_ref = quarter.reshape(D, HEADS_WIDTH)
     grad_ref[...] = dot(branch_ref[...], weight_ref[:, 4 * HD :]).astype(LOW)
     query_terms, key_terms = 0.0, 0.0
     for b in range(raw_ref.shape[0] // SEQ):
@@ -232,16 +277,11 @@
 def iterate_kernel(*refs):
     pieces, out_ref, refs = refs[:8], refs[8], refs[9:]
     quarters, gram, high, low, poly, mixed_high, mixed_low, own, arrived = refs[:4], *refs[4:]
-    copies = []
-    for i in range(4):
-        for part in range(2):
-            place = [slice(None)] * 4
-            place[(3 + i) % 4] = slice(part, part + 1)
-            copies.append(
-                pltpu.make_async_copy(
-                    pieces[2 * i + part], quarters[i].at[tuple(place)], arrived.at[2 * i + part]
-                )
-            )
+    copies = [
+        copy
+        for i in range(4)
+        for copy in fetch(pieces[2 * i : 2 * i + 2], quarters[i], arrived.at[i], (3 + i) % 4)
+    ]
     for copy in copies:
         copy.start()
     for copy in copies:
@@ -343,9 +383,9 @@
             pltpu.VMEM((D, D), F32),
             *[square] * 5,
             pltpu.VMEM((64, D), F32),
-            pltpu.SemaphoreType.DMA((8,)),
+            pltpu.SemaphoreType.DMA((4, 2)),
         ],
-        compiler_params=pltpu.CompilerParams(vmem_limit_bytes=48 * 2**20),
+        compiler_params=pltpu.CompilerParams(vmem_limit_bytes=32 * 2**20),
         cost_estimate=pl.CostEstimate(flops=50 * 10**9, bytes_accessed=2**23, transcendentals=0),
     )(*pieces)
 
@@ -359,17 +399,25 @@
 
 
 SMALL = pl.CostEstimate(flops=2**20, bytes_accessed=2**16, transcendentals=0)
-KERNEL_SPACE = pltpu.CompilerParams(vmem_limit_bytes=32 * 2**20)
-
-
-def heads_forward(inputs, weight, cosine, sine, gain_rows, total):
+KERNEL_SPACE = pltpu.CompilerParams(vmem_limit_bytes=16 * 2**20)
+
+
+AS_IT_LIES = pl.BlockSpec(memory_space=pl.ANY)
+HEADS_SCRATCH = [
+    pltpu.VMEM((2, 2, 2, 2, D // 16, 6 * HD), LOW),
+    pltpu.SemaphoreType.DMA((2,)),
+]
+
+
+def heads_forward(link, inputs, weight, cosine, sine, gain_rows, total):
     tokens = inputs.shape[0]
     return pl.pallas_call(
-        heads_kernel,
+        functools.partial(heads_kernel, link),
         grid=(tokens // (2 * SEQ),),
         in_specs=[
             by_sequence(D),
-            whole(D, 6 * HD),
+            AS_IT_LIES,
+            AS_IT_LIES,
             by_sequence(HD),
             by_sequence(HD),
             whole(8, HD),
@@ -381,20 +429,22 @@
             jax.ShapeDtypeStruct((tokens, 2 * HD), LOW),
             jax.ShapeDtypeStruct((tokens, D), F32),
         ],
+        scratch_shapes=HEADS_SCRATCH,
         compiler_params=KERNEL_SPACE,
         cost_estimate=SMALL,
-    )(inputs, weight, cosine, sine, gain_rows, total)
-
-
-def heads_backward(raw, branch, weight, cosine, sine, gain_rows, total):
+    )(inputs, *weight, cosine, sine, gain_rows, total)
+
+
+def heads_backward(link, raw, branch, weight, cosine, sine, gain_rows, total):
     tokens = raw.shape[0]
     grad_raw, terms, total = pl.pallas_call(
-        heads_back_kernel,
+        functools.partial(heads_back_kernel, link),
         grid=(tokens // (2 * SEQ),),
         in_specs=[
             by_sequence(4 * HD),
             by_sequence(D),
-            whole(D, 6 * HD),
+            AS_IT_LIES,
+            AS_IT_LIES,
             by_sequence(HD),
             by_sequence(HD),
             whole(8, HD),
@@ -410,19 +460,28 @@
             jax.ShapeDtypeStruct((tokens // (2 * SEQ) * 8, HD), F32),
             jax.ShapeDtypeStruct((tokens, D), F32),
         ],
-        scratch_shapes=[pltpu.VMEM((2 * SEQ, 2 * HD), LOW)],
+        scratch_shapes=[pltpu.VMEM((2 * SEQ, 2 * HD), LOW), *HEADS_SCRATCH],
         compiler_params=KERNEL_SPACE,
         cost_estimate=SMALL,
-    )(raw, branch, weight, cosine, sine, gain_rows, total)
+    )(raw, branch, *weight, cosine, sine, gain_rows, total)
     return grad_raw, jnp.sum(terms.reshape(-1, 8, HD), axis=0), total
 
 
-def inner_kernel(
-    input_ref, grad_ref, w0, w1, w2, w3, act_ref, inner_ref, outward_ref, back_ref
-):
+def inner_kernel(input_ref, grad_ref, *refs):
+    pieces, (act_ref, inner_ref), sums = refs[:8], refs[8:10], refs[10:14]
+    quarters, arrived = refs[14:18], refs[18]
+    copies = [
+        fetch(pieces[2 * i : 2 * i + 2], quarters[i], arrived.at[i], (3 + i) % 4) for i in range(4)
+    ]
+    for pair in copies:
+        for copy in pair:
+            copy.start()
     width = FF // 8
     outward, back = 0.0, 0.0
-    for i, w in enumerate((w0, w1, w2, w3)):
+    for i in range(4):
+        for copy in copies[i]:
+            copy.wait()
+        w = quarters[i].reshape(D, INNER_WIDTH)
         gate_up = dot(input_ref[...], w[:, : 2 * width])
         gate, up = gate_up[:, :width], gate_up[:, width:]
         sigmoid = jax.nn.sigmoid(gate)
@@ -436,25 +495,36 @@
         inner_ref[:, start + width : start + 2 * width] = (grad_act * swish).astype(LOW)
         outward = outward + dot(act, w[:, 2 * width :], LAST)
         back = back + dot(inner_ref[:, start : start + 2 * width], w[:, : 2 * width], LAST)
-    outward_ref[...] = outward
-    back_ref[...] = back
-
-
-def inner_units(inputs, grads, weights):
+    own = outward.shape[0] // 2
+    for total, own_ref, other_ref in ((outward, *sums[:2]), (back, *sums[2:])):
+        own_ref[...] = total[:own]
+        other_ref[...] = total[own:].astype(LOW)
+
+
+def inner_units(inputs, grads, pieces):
     tokens = inputs.shape[0]
+    in_vmem = pl.BlockSpec(memory_space=pltpu.VMEM)
+    halves = [
+        jax.ShapeDtypeStruct((tokens // 2, D), F32),
+        jax.ShapeDtypeStruct((tokens // 2, D), LOW),
+    ]
     return pl.pallas_call(
         inner_kernel,
-        in_specs=[pl.BlockSpec(memory_space=pltpu.VMEM)] * 6,
-        out_specs=[pl.BlockSpec(memory_space=pltpu.VMEM)] * 4,
+        in_specs=[in_vmem] * 2 + [AS_IT_LIES] * 8,
+        out_specs=[in_vmem] * 6,
         out_shape=[
             jax.ShapeDtypeStruct((tokens, FF // 2), LOW),
             jax.ShapeDtypeStruct((tokens, FF), LOW),
-            jax.ShapeDtypeStruct((tokens, D), F32),
-            jax.ShapeDtypeStruct((tokens, D), F32),
+            *halves,
+            *halves,
         ],
-        compiler_params=pltpu.CompilerParams(vmem_limit_bytes=48 * 2**20),
+        scratch_shapes=[
+            *[pltpu.VMEM((2, 2, 2, 2, D // 16, INNER_WIDTH), LOW)] * 4,
+            pltpu.SemaphoreType.DMA((4, 2)),
+        ],
+        compiler_params=pltpu.CompilerParams(vmem_limit_bytes=36 * 2**20),
         cost_estimate=SMALL,
-    )(inputs, grads, *weights)
+    )(inputs, grads, *pieces)
 
 
 def terms_kernel(link, first_left, first_right, second_left, second_right, kept_ref, sent_ref):
@@ -670,13 +740,17 @@
     heads_held = together(gather_step(heads_held, 0))
     held = together([*gather_step(heads_held, 1), *gather_step(inner_held, 0)])
     held = together([*gather_step(held[:4], 2), *gather_step(held[4:], 1)])
-    held = together([*gather_step(held[:4], 3), *gather_step(held[4:], 2)])
-    w_heads = flat(held[:4])
-    w_inner = flat(gather_step(held[4:], 3))
+    heads_held, inner_held = held[:4], held[4:]
+    held = together([*gather_came(heads_held, 3), *gather_step(inner_held, 2)])
+    w_heads = list(zip(heads_held, held[:4]))
+    inner_held = held[4:]
+    w_inner = [x for pair in zip(inner_held, gather_came(inner_held, 3)) for x in pair]
     raw, attn = [], []
     branch = jnp.zeros((2 * tok_count, D), F32)
-    for w in w_heads:
-        fresh, heads, branch = heads_forward(input_one, w, cosine, sine, gain_rows, branch)
+    for i in range(4):
+        fresh, heads, branch = heads_forward(
+            (3 + i) % 4, input_one, w_heads[i], cosine, sine, gain_rows, branch
+        )
         raw.append(fresh)
         attn.append(heads)
     *w_inner, branch = together([*w_inner, branch])
@@ -684,8 +758,10 @@
     scale_two = lax.rsqrt(jnp.mean(residual * residual, axis=-1, keepdims=True) + norm_eps)
     normed_two = residual * scale_two
     input_two = both((normed_two * gain_two).astype(LOW))
-    act, grad_inner, outward, grad_two = inner_units(input_two, grad_low, w_inner)
-    result = (residual + shared_sum(outward)) * live_token
+    act, grad_inner, outward, outward_other, grad_two, grad_two_other = inner_units(
+        input_two, grad_low, w_inner
+    )
+    result = (residual + (outward + swap(outward_other).astype(F32))) * live_token
     hidden_out = dot(result.astype(LOW), reorder, LAST).astype(LOW)
 
     sent, kept = [], []
@@ -695,7 +771,7 @@
         )
         sent.append(send)
         kept.append(keep)
-    grad_two = shared_sum(grad_two)
+    grad_two = grad_two + swap(grad_two_other).astype(F32)
     gain_two_term = jnp.sum(grad_two * normed_two, axis=0, keepdims=True)
     grad_residual = grad_out + norm_back(grad_two * gain_two, normed_two, scale_two)
     branch_low = both(grad_residual.astype(LOW))
@@ -704,7 +780,7 @@
 
     def back_through(i, branch, grad_one):
         fresh, term, grad_one = heads_backward(
-            raw[i], branch, w_heads[i], cosine, sine, gain_rows, grad_one
+            (3 + i) % 4, raw[i], branch, w_heads[i], cosine, sine, gain_rows, grad_one
         )
         grad_raw.append(fresh)
         return head_terms + term, grad_one
@@ -827,12 +903,14 @@
 
     gain_momentum_new = momentum_keep * gain_momentum + gain_grad
     gain_step = gain_grad + momentum_keep * gain_momentum_new
-    bounds = (0, D, 2 * D, 2 * D + HD, 2 * D + 2 * HD)
-    scaled_parts = []
-    for number in range(4):
-        segment = gain_step[bounds[number] : bounds[number + 1]]
-        scaled_parts.append(segment * lax.rsqrt(jnp.mean(segment * segment) + norm_eps))
-    gain_new = gains - gain_rate * jnp.concatenate(scaled_parts)
+    rows = gain_step.reshape(18, HD)
+    part = jnp.minimum(jnp.arange(18) // 8, 1) + (jnp.arange(18) // 16) * (jnp.arange(18) - 15)
+    alike = part[:, None] == part[None, :]
+    squares = jnp.sum(rows * rows, axis=1)
+    sums = jnp.sum(jnp.where(alike, squares[None, :], 0.0), axis=1, keepdims=True)
+    counts = jnp.sum(jnp.where(alike, float(HD), 0.0), axis=1, keepdims=True)
+    scaled = rows * lax.rsqrt(sums / counts + norm_eps)
+    gain_new = gains - gain_rate * scaled.reshape(-1)
     shape = (slot_count, length, D)
     return (
         hidden_out.reshape(shape),

time: 470 us -> 452 us (0.962)
  other arithmetic: 32 us -> 19.7 us
    concatenate x42 -> x36, other arithmetic: 9.19 us -> 1.99 us  [gather_step(): jnp.concatenate([quarters[i], fresh[i]], axis=(step + i) % 4)]
    unnamed x98 -> x102, local copies, waits for them, and re-layouts: 11.9 us -> 13.6 us
  transfers between devices with their start and end apart: 104 -> 104, of which waited for: 58 -> 59; matrix products, arithmetic and copies ran while one was open for 5% -> 6% of each run, Pallas kernels for 12% -> 12%
where the time goes in v1:
time: 452 us; the launch traced here: 443 us
  starting transfers between devices  143 us (32%)
  waiting for transfers between devices  131 us (29%)
  Pallas kernels  116 us (26%)
  other arithmetic  19.7 us (4%)
  local copies, waits for them, and re-layouts  15.6 us (3%)
  matrix products  14.2 us (3%)
    ppermute x48, waiting for transfers between devices, gather_came(): fresh.append(lax.ppermute(quarters[i], axis, pairs))  59.1 us
    ppermute x14, starting transfers between devices, swap(): return lax.ppermute(x, 'dp_2', ((0, 1), (1, 0)))  55.2 us
    pallas_call x1, Pallas kernels, iterate_rows(): pl.pallas_call(iterate_kernel, in_specs=[pl.BlockSpec(memory_space=pl.ANY...  45.8 us
    ppermute x48, starting transfers between devices, gather_came(): fresh.append(lax.ppermute(quarters[i], axis, pairs))  45.7 us
    ppermute x32, waiting for transfers between devices, scatter_step(): came.append(lax.ppermute(sent[i], axis, pairs))  40.8 us
    ppermute x32, starting transfers between devices, scatter_step(): came.append(lax.ppermute(sent[i], axis, pairs))  28.6 us
    pallas_call x4, Pallas kernels, heads_backward(): pl.pallas_call(functools.partial(heads_back_kernel, link), grid=(tokens /...  21.6 us
    pallas_call x8, Pallas kernels, terms(): pl.pallas_call(functools.partial(terms_kernel, link), grid=(4,), in_specs...  19.3 us
  transfers between devices with their start and end apart: 104, of which 59 were waited for; matrix products, arithmetic and copies ran while one was open for 6% of the time, Pallas kernels for 12%

profile of v1, /device:TPU:1, one launch (start us, length us, event | category | flops | bytes accessed | tf_op | source)
XLA Modules:
  0.0 442.6 jit_solution(1182564956432059935)
XLA Ops:
  12.9 6.7 %collective-permute-done.3 = bf16[1,2,2,16,3072]{4,3,2,1,0:T(8,128)(2,1)S(1)} collective-permute-done((bf16[1,2,2,16,3072]{4,3,2,1,0:T(8,128)(2,1)S(1)}, bf16[1,2,2,16,3072]{4,3,2,1,0:T(8,128)(2,1)S(1)}, u32[]{:S(2)}, u32[]{:S(2)}) %collective-permute-start.3) | collective-permute-done | bytes 393248 | tf_op jit(solution)/shard_map/ppermute | solution.py:103
  21.7 2.9 collective-permute-start.4
  52.0 3.7 collective-permute-done.21
  58.9 8.5 %collective-permute-done.17 = bf16[2,2,1,1,64,768]{5,4,3,2,1,0:T(8,128)(2,1)S(1)} collective-permute-done((bf16[2,2,1,1,64,768]{5,4,3,2,1,0:T(8,128)(2,1)S(1)}, bf16[2,2,1,1,64,768]{5,4,3,2,1,0:T(8,128)(2,1)S(1)}, u32[]{:S(2)}, u32[]{:S(2)}) %collective-permute-start.17) | collective-permute-done | bytes 393248 | tf_op jit(solution)/shard_map/ppermute | solution.py:58
  73.8 4.2 collective-permute-done.29
  83.4 13.0 %collective-permute-done.25.fresh_ref = bf16[2,2,2,1,64,768]{5,4,3,2,1,0:T(8,128)(2,1)S(1)} collective-permute-done((bf16[2,2,2,1,64,768]{5,4,3,2,1,0:T(8,128)(2,1)S(1)}, bf16[2,2,2,1,64,768]{5,4,3,2,1,0:T(8,128)(2,1)S(1)}, u32[]{:S(2)}, u32[]{:S(2)}) %collective-permute-start.25) | collective-permute-done | bytes 786464 | tf_op jit(solution)/shard_map/ppermute | solution.py:58
  103.2 20.6 %collective-permute-start.37 = (bf16[256,1024]{1,0:T(8,128)(2,1)S(1)}, bf16[256,1024]{1,0:T(8,128)(2,1)S(1)}, u32[]{:S(2)}, u32[]{:S(2)}) collective-permute-start(bf16[256,1024]{1,0:T(8,128)(2,1)S(1)} %multiply_convert_fusion.2), channel_id=1, source_target_pairs={{0,4},{4,0},{1,5},{5,1},{2,6},{6,2},{3,7},{7,3},{8,12},{12,8},{9,1... | collective-permute-start | bytes 1572872 | tf_op jit(solution)/shard_map/ppermute | solution.py:47
  125.7 3.0 shard_map.171
  129.6 3.0 shard_map.172
  132.6 3.0 shard_map.173
  136.5 3.0 shard_map.174
  145.2 16.1 %shard_map.175 = (bf16[512,1536]{1,0:T(8,128)(2,1)S(1)}, bf16[512,3072]{1,0:T(8,128)(2,1)}, f32[256,1024]{1,0:T(8,128)S(1)}, bf16[256,1024]{1,0:T(8,128)(2,1)S(1...) custom-call(bf16[512,1024]{1,0:T(8,128)(2,1)S(1)} %pad_maximum_fusion.5.input_ref.first_left, ...), custom_call_target="tpu_custom_call" | custom-call | flops 1048576 | bytes 65536 | tf_op jit(solution)/shard_map/pallas_call | solution.py:511
  171.7 2.8 shard_map.178
  175.4 2.9 shard_map.177
  182.5 5.4 %shard_map.176 = (bf16[512,512]{1,0:T(8,128)(2,1)S(1)}, f32[16,128]{1,0:T(8,128)S(1)}, f32[512,1024]{1,0:T(8,128)S(1)}) custom-call(f32[512,512]{1,0:T(8,128)S(1)} %copy-done.10, bf16[512,1024]{1,0:T(8,128)(2,1)S(1)} %pad_maximum_fusion.7.branch_ref.second_left, bf16[2,2,2,1,64,768]{5,4,3,2,1,0:T(8,128)(2,1)S(1)} %pad_maximum_fusion.11.held_ref, ...), custom_call_target="tpu_custom_call" | custom-call | flops 1048576 | bytes 65536 | tf_op jit(solution)/shard_map/pallas_call | solution.py:440
  187.9 5.4 %shard_map.181 = (bf16[512,512]{1,0:T(8,128)(2,1)S(1)}, f32[16,128]{1,0:T(8,128)S(1)}, f32[512,1024]{1,0:T(8,128)S(1)}) custom-call(f32[512,512]{1,0:T(8,128)S(1)} %copy-done.8, bf16[512,1024]{1,0:T(8,128)(2,1)S(1)} %pad_maximum_fusion.7.branch_ref.second_left, bf16[1,2,2,2,64,768]{5,4,3,2,1,0:T(8,128)(2,1)S(1)} %pad_maximum_fusion.12.held_ref, ...), custom_call_target="tpu_custom_call" | custom-call | flops 1048576 | bytes 65536 | tf_op jit(solution)/shard_map/pallas_call | solution.py:440
  194.8 4.2 collective-permute-done.47
  201.1 3.4 collective-permute-done.45
  209.5 5.4 %shard_map.183 = (bf16[512,512]{1,0:T(8,128)(2,1)S(1)}, f32[16,128]{1,0:T(8,128)S(1)}, f32[512,1024]{1,0:T(8,128)S(1)}) custom-call(f32[512,512]{1,0:T(8,128)S(1)} %copy-done.6, bf16[512,1024]{1,0:T(8,128)(2,1)S(1)} %pad_maximum_fusion.7.branch_ref.second_left, bf16[2,1,2,2,64,768]{5,4,3,2,1,0:T(8,128)(2,1)S(1)} %pad_maximum_fusion.13.held_ref, ...), custom_call_target="tpu_custom_call" | custom-call | flops 1048576 | bytes 65536 | tf_op jit(solution)/shard_map/pallas_call | solution.py:440
  225.1 5.4 %shard_map.185 = (bf16[512,512]{1,0:T(8,128)(2,1)S(1)}, f32[16,128]{1,0:T(8,128)S(1)}, f32[512,1024]{1,0:T(8,128)S(1)}) custom-call(f32[512,512]{1,0:T(8,128)S(1)} %copy-done.4, bf16[512,1024]{1,0:T(8,128)(2,1)S(1)} %pad_maximum_fusion.7.branch_ref.second_left, bf16[2,2,1,2,64,768]{5,4,3,2,1,0:T(8,128)(2,1)S(1)} %pad_maximum_fusion.14.held_ref, ...), custom_call_target="tpu_custom_call" | custom-call | flops 1048576 | bytes 65536 | tf_op jit(solution)/shard_map/pallas_call | solution.py:440
  241.3 5.4 %collective-permute-start.61 = (bf16[256,1024]{1,0:T(8,128)(2,1)S(1)}, bf16[256,1024]{1,0:T(8,128)(2,1)S(1)}, u32[]{:S(2)}, u32[]{:S(2)}) collective-permute-start(bf16[256,1024]{1,0:T(8,128)(2,1)S(1)} %slice.773), channel_id=1, source_target_pairs={{0,4},{4,0},{1,5},{5,1},{2,6},{6,2},{3,7},{7,3},{8,12},{12,8},{9,1... | collective-permute-start | bytes 1572872 | tf_op jit(solution)/shard_map/ppermute | solution.py:47
  255.0 11.0 %collective-permute-done.58 = bf16[2,1,2,2,64,768]{5,4,3,2,1,0:T(8,128)(2,1)S(1)} collective-permute-done((bf16[2,1,2,2,64,768]{5,4,3,2,1,0:T(8,128)(2,1)S(1)}, bf16[2,1,2,2,64,768]{5,4,3,2,1,0:T(8,128)(2,1)S(1)}, u32[]{:S(2)}, u32[]{:S(2)}) %collective-permute-start.58) | collective-permute-done | bytes 786464 | tf_op jit(solution)/shard_map/ppermute | solution.py:83
  272.8 4.0 collective-permute-done.62
  300.2 6.2 %collective-permute-start.81 = (bf16[32,7680]{1,0:T(8,128)(2,1)S(1)}, bf16[32,7680]{1,0:T(8,128)(2,1)S(1)}, u32[]{:S(2)}, u32[]{:S(2)}) collective-permute-start(bf16[32,7680]{1,0:T(8,128)(2,1)S(1)} %get-tuple-element.559), channel_id=1, source_target_pairs={{0,4},{4,0},{1,5},{5,1},{2,6},{6,2},{3,7},{7,3},{8,12},{12,8},{9,1... | collective-permute-start | bytes 1474568 | tf_op jit(solution)/shard_map/ppermute | solution.py:47
  312.1 7.0 %collective-permute-done.82 = bf16[4,16,3072]{2,1,0:T(8,128)(2,1)S(1)} collective-permute-done((bf16[4,16,3072]{2,1,0:T(8,128)(2,1)S(1)}, bf16[4,16,3072]{2,1,0:T(8,128)(2,1)S(1)}, u32[]{:S(2)}, u32[]{:S(2)}) %collective-permute-start.82) | collective-permute-done | bytes 393248 | tf_op jit(solution)/shard_map/ppermute | solution.py:854
  323.6 4.2 collective-permute-done.84
  329.8 2.7 collective-permute-start.86
  344.0 2.8 collective-permute-done.92
  351.7 4.5 %collective-permute-start.42 = (bf16[256,1024]{1,0:T(8,128)(2,1)S(1)}, bf16[256,1024]{1,0:T(8,128)(2,1)S(1)}, u32[]{:S(2)}, u32[]{:S(2)}) collective-permute-start(bf16[256,1024]{1,0:T(8,128)(2,1)S(1)} %copy-done.28), channel_id=1, source_target_pairs={{0,4},{4,0},{1,5},{5,1},{2,6},{6,2},{3,7},{7,3},{8,12},{12,8},{9,1... | collective-permute-start | bytes 1572872 | tf_op jit(solution)/shard_map/ppermute | solution.py:47
  365.4 9.0 %collective-permute-done.100.refs_3_ = bf16[1,2,2,2,64,768]{5,4,3,2,1,0:T(8,128)(2,1)S(1)} collective-permute-done((bf16[1,2,2,2,64,768]{5,4,3,2,1,0:T(8,128)(2,1)S(1)}, bf16[1,2,2,2,64,768]{5,4,3,2,1,0:T(8,128)(2,1)S(1)}, u32[]{:S(2)}, u32[]{:S(2)}) %collective-permute-start.100) | collective-permute-done | bytes 786464 | tf_op jit(solution)/shard_map/ppermute | solution.py:58
  387.7 45.8 %shard_map.189 = bf16[64,3072]{1,0:T(8,128)(2,1)S(1)} custom-call(bf16[2,2,2,1,64,896]{5,4,3,2,1,0:T(8,128)(2,1)S(1)} %pad_maximum_fusion.8.refs_0_, bf16[2,2,2,1,64,896]{5,4,3,2,1,0:T(8,128)(2,1)S(1)} %copy-done.18, bf16[1,2,2,2,64,768]{5,4,3,2,1,0:T(8,128)(2,1)S(1)} %copy-done.12, bf16[1,2,2,2,64,768]{5,4,3,2,1,0:T(8,128)(2,1)S(1)} %copy-done.22, ...), custom_call_target="tpu_custom_call" | custom-call | flops 49999998976 | bytes 8388608 | tf_op jit(solution)/shard_map/pallas_call | solution.py:376
  433.6 6.4 %collective-permute-start.103 = (bf16[32,3072]{1,0:T(8,128)(2,1)S(1)}, bf16[32,3072]{1,0:T(8,128)(2,1)S(1)}, u32[]{:S(2)}, u32[]{:S(2)}) collective-permute-start(bf16[32,3072]{1,0:T(8,128)(2,1)S(1)} %broadcast_select_fusion.2), channel_id=1, source_target_pairs={{0,4},{4,0},{1,5},{5,1},{2,6},{6,2},{3,7},{7,3},{8,12},{12,8},{9,1... | collective-permute-start | bytes 589832 | tf_op jit(solution)/shard_map/ppermute | solution.py:47
  (475 shorter events, 208.4 us)
Async XLA Ops:
  5.9 97.3 %collective-permute-start.38 = (s32[2,128]{1,0:T(2,128)}, s32[2,128]{1,0:T(2,128)S(1)}, u32[]{:S(2)}, u32[]{:S(2)}) collective-permute-start(s32[2,128]{1,0:T(2,128)} %param.14), channel_id=1, source_target_pairs={{0,4},{4,0},{1,5},{5,1},{2,6},{6,2},{3,7},{7,3},{8,12},{12,8},{9,1... | collective-permute-start | bytes 3080 | tf_op jit(solution)/shard_map/ppermute | solution.py:47
  55.7 11.7 %collective-permute-start.17 = (bf16[2,2,1,1,64,768]{5,4,3,2,1,0:T(8,128)(2,1)S(1)}, bf16[2,2,1,1,64,768]{5,4,3,2,1,0:T(8,128)(2,1)S(1)}, u32[]{:S(2)}, u32[]{:S(2)}) collective-permute-start(bf16[2,2,1,1,64,768]{5,4,3,2,1,0:T(8,128)(2,1)S(1)} %pad_maximum_fusion.26), channel_id=1, source_target_pairs={{0,96},{96,0},{32,64},{64,32},{1,97},{97,1},{33,65},{65,33},{2,98}... | collective-permute-start | bytes 1179656 | tf_op jit(solution)/shard_map/ppermute | solution.py:58
  78.1 18.3 %collective-permute-start.25 = (bf16[2,2,2,1,64,768]{5,4,3,2,1,0:T(8,128)(2,1)S(1)}, bf16[2,2,2,1,64,768]{5,4,3,2,1,0:T(8,128)(2,1)S(1)}, u32[]{:S(2)}, u32[]{:S(2)}) collective-permute-start(bf16[2,2,2,1,64,768]{5,4,3,2,1,0:T(8,128)(2,1)S(1)} %pad_maximum_fusion.11.held_ref), channel_id=1, source_target_pairs={{0,24},{24,0},{8,16},{16,8},{1,25},{25,1},{9,17},{17,9},{2,26},{26... | collective-permute-start | bytes 2359304 | tf_op jit(solution)/shard_map/ppermute | solution.py:58
  80.5 16.2 %collective-permute-start.26 = (bf16[1,2,2,2,64,768]{5,4,3,2,1,0:T(8,128)(2,1)S(1)}, bf16[1,2,2,2,64,768]{5,4,3,2,1,0:T(8,128)(2,1)S(1)}, u32[]{:S(2)}, u32[]{:S(2)}) collective-permute-start(bf16[1,2,2,2,64,768]{5,4,3,2,1,0:T(8,128)(2,1)S(1)} %pad_maximum_fusion.12.held_ref), channel_id=1, source_target_pairs={{0,32},{32,0},{64,96},{96,64},{1,33},{33,1},{65,97},{97,65},{2,34}... | collective-permute-start | bytes 2359304 | tf_op jit(solution)/shard_map/ppermute | solution.py:58
  81.1 17.2 %collective-permute-start.27 = (bf16[2,1,2,2,64,768]{5,4,3,2,1,0:T(8,128)(2,1)S(1)}, bf16[2,1,2,2,64,768]{5,4,3,2,1,0:T(8,128)(2,1)S(1)}, u32[]{:S(2)}, u32[]{:S(2)}) collective-permute-start(bf16[2,1,2,2,64,768]{5,4,3,2,1,0:T(8,128)(2,1)S(1)} %pad_maximum_fusion.13.held_ref), channel_id=1, source_target_pairs={{0,8},{8,0},{16,24},{24,16},{1,9},{9,1},{17,25},{25,17},{2,10},{10... | collective-permute-start | bytes 2359304 | tf_op jit(solution)/shard_map/ppermute | solution.py:58
  82.1 16.1 %collective-permute-start.28 = (bf16[2,2,1,2,64,768]{5,4,3,2,1,0:T(8,128)(2,1)S(1)}, bf16[2,2,1,2,64,768]{5,4,3,2,1,0:T(8,128)(2,1)S(1)}, u32[]{:S(2)}, u32[]{:S(2)}) collective-permute-start(bf16[2,2,1,2,64,768]{5,4,3,2,1,0:T(8,128)(2,1)S(1)} %pad_maximum_fusion.14.held_ref), channel_id=1, source_target_pairs={{0,96},{96,0},{32,64},{64,32},{1,97},{97,1},{33,65},{65,33},{2,98}... | collective-permute-start | bytes 2359304 | tf_op jit(solution)/shard_map/ppermute | solution.py:58
  98.3 41.3 %collective-permute-start.33 = (bf16[2,2,2,1,64,1152]{5,4,3,2,1,0:T(8,128)(2,1)S(1)}, bf16[2,2,2,1,64,1152]{5,4,3,2,1,0:T(8,128)(2,1)S(1)}, u32[]{:S(2)}, u32[]{:S(2)}) collective-permute-start(bf16[2,2,2,1,64,1152]{5,4,3,2,1,0:T(8,128)(2,1)S(1)} %pad_maximum_fusion.refs_0_), channel_id=1, source_target_pairs={{0,24},{24,0},{8,16},{16,8},{1,25},{25,1},{9,17},{17,9},{2,26},{26... | collective-permute-start | bytes 3538952 | tf_op jit(solution)/shard_map/ppermute | solution.py:58
  100.4 39.1 %collective-permute-start.34 = (bf16[1,2,2,2,64,1152]{5,4,3,2,1,0:T(8,128)(2,1)S(1)}, bf16[1,2,2,2,64,1152]{5,4,3,2,1,0:T(8,128)(2,1)S(1)}, u32[]{:S(2)}, u32[]{:S(2)}) collective-permute-start(bf16[1,2,2,2,64,1152]{5,4,3,2,1,0:T(8,128)(2,1)S(1)} %pad_maximum_fusion.1.refs_2_), channel_id=1, source_target_pairs={{0,32},{32,0},{64,96},{96,64},{1,33},{33,1},{65,97},{97,65},{2,34}... | collective-permute-start | bytes 3538952 | tf_op jit(solution)/shard_map/ppermute | solution.py:58
  101.1 38.4 %collective-permute-start.35 = (bf16[2,1,2,2,64,1152]{5,4,3,2,1,0:T(8,128)(2,1)S(1)}, bf16[2,1,2,2,64,1152]{5,4,3,2,1,0:T(8,128)(2,1)S(1)}, u32[]{:S(2)}, u32[]{:S(2)}) collective-permute-start(bf16[2,1,2,2,64,1152]{5,4,3,2,1,0:T(8,128)(2,1)S(1)} %pad_maximum_fusion.2.refs_4_), channel_id=1, source_target_pairs={{0,8},{8,0},{16,24},{24,16},{1,9},{9,1},{17,25},{25,17},{2,10},{10... | collective-permute-start | bytes 3538952 | tf_op jit(solution)/shard_map/ppermute | solution.py:58
  101.1 38.5 %collective-permute-start.36 = (bf16[2,2,1,2,64,1152]{5,4,3,2,1,0:T(8,128)(2,1)S(1)}, bf16[2,2,1,2,64,1152]{5,4,3,2,1,0:T(8,128)(2,1)S(1)}, u32[]{:S(2)}, u32[]{:S(2)}) collective-permute-start(bf16[2,2,1,2,64,1152]{5,4,3,2,1,0:T(8,128)(2,1)S(1)} %pad_maximum_fusion.3.refs_6_), channel_id=1, source_target_pairs={{0,96},{96,0},{32,64},{64,32},{1,97},{97,1},{33,65},{65,33},{2,98}... | collective-permute-start | bytes 3538952 | tf_op jit(solution)/shard_map/ppermute | solution.py:58
  103.2 22.2 %collective-permute-start.37 = (bf16[256,1024]{1,0:T(8,128)(2,1)S(1)}, bf16[256,1024]{1,0:T(8,128)(2,1)S(1)}, u32[]{:S(2)}, u32[]{:S(2)}) collective-permute-start(bf16[256,1024]{1,0:T(8,128)(2,1)S(1)} %multiply_convert_fusion.2), channel_id=1, source_target_pairs={{0,4},{4,0},{1,5},{5,1},{2,6},{6,2},{3,7},{7,3},{8,12},{12,8},{9,1... | collective-permute-start | bytes 1572872 | tf_op jit(solution)/shard_map/ppermute | solution.py:47
  161.3 17.0 %collective-permute-start.43 = (bf16[256,1024]{1,0:T(8,128)(2,1)S(1)}, bf16[256,1024]{1,0:T(8,128)(2,1)S(1)}, u32[]{:S(2)}, u32[]{:S(2)}) collective-permute-start(bf16[256,1024]{1,0:T(8,128)(2,1)S(1)} %get-tuple-element.346), channel_id=1, source_target_pairs={{0,4},{4,0},{1,5},{5,1},{2,6},{6,2},{3,7},{7,3},{8,12},{12,8},{9,1... | collective-permute-start | bytes 1572872 | tf_op jit(solution)/shard_map/ppermute | solution.py:47
  166.4 28.4 %collective-permute-start.48 = (bf16[2,2,2,1,64,1152]{5,4,3,2,1,0:T(8,128)(2,1)S(1)}, bf16[2,2,2,1,64,1152]{5,4,3,2,1,0:T(8,128)(2,1)S(1)}, u32[]{:S(2)}, u32[]{:S(2)}) collective-permute-start(bf16[2,2,2,1,64,1152]{5,4,3,2,1,0:T(8,128)(2,1)S(1)} %bitcast.145), channel_id=1, source_target_pairs={{0,24},{24,0},{8,16},{16,8},{1,25},{25,1},{9,17},{17,9},{2,26},{26... | collective-permute-start | bytes 3538952 | tf_op jit(solution)/shard_map/ppermute | solution.py:83
  170.7 28.3 %collective-permute-start.47 = (bf16[2,2,1,2,64,1152]{5,4,3,2,1,0:T(8,128)(2,1)S(1)}, bf16[2,2,1,2,64,1152]{5,4,3,2,1,0:T(8,128)(2,1)S(1)}, u32[]{:S(2)}, u32[]{:S(2)}) collective-permute-start(bf16[2,2,1,2,64,1152]{5,4,3,2,1,0:T(8,128)(2,1)S(1)} %bitcast.146), channel_id=1, source_target_pairs={{0,96},{96,0},{32,64},{64,32},{1,97},{97,1},{33,65},{65,33},{2,98}... | collective-permute-start | bytes 3538952 | tf_op jit(solution)/shard_map/ppermute | solution.py:83
  174.5 26.6 %collective-permute-start.46 = (bf16[2,1,2,2,64,1152]{5,4,3,2,1,0:T(8,128)(2,1)S(1)}, bf16[2,1,2,2,64,1152]{5,4,3,2,1,0:T(8,128)(2,1)S(1)}, u32[]{:S(2)}, u32[]{:S(2)}) collective-permute-start(bf16[2,1,2,2,64,1152]{5,4,3,2,1,0:T(8,128)(2,1)S(1)} %bitcast.147), channel_id=1, source_target_pairs={{0,8},{8,0},{16,24},{24,16},{1,9},{9,1},{17,25},{25,17},{2,10},{10... | collective-permute-start | bytes 3538952 | tf_op jit(solution)/shard_map/ppermute | solution.py:83
  178.2 26.3 %collective-permute-start.45 = (bf16[1,2,2,2,64,1152]{5,4,3,2,1,0:T(8,128)(2,1)S(1)}, bf16[1,2,2,2,64,1152]{5,4,3,2,1,0:T(8,128)(2,1)S(1)}, u32[]{:S(2)}, u32[]{:S(2)}) collective-permute-start(bf16[1,2,2,2,64,1152]{5,4,3,2,1,0:T(8,128)(2,1)S(1)} %bitcast.148), channel_id=1, source_target_pairs={{0,32},{32,0},{64,96},{96,64},{1,33},{33,1},{65,97},{97,65},{2,34}... | collective-permute-start | bytes 3538952 | tf_op jit(solution)/shard_map/ppermute | solution.py:83
  205.7 12.7 %collective-permute-start.49 = (bf16[1,1,2,2,64,1152]{5,4,3,2,1,0:T(8,128)(2,1)S(1)}, bf16[1,1,2,2,64,1152]{5,4,3,2,1,0:T(8,128)(2,1)S(1)}, u32[]{:S(2)}, u32[]{:S(2)}) collective-permute-start(bf16[1,1,2,2,64,1152]{5,4,3,2,1,0:T(8,128)(2,1)S(1)} %get-tuple-element.369), channel_id=1, source_target_pairs={{0,8},{8,0},{16,24},{24,16},{1,9},{9,1},{17,25},{25,17},{2,10},{10... | collective-permute-start | bytes 1769480 | tf_op jit(solution)/shard_map/ppermute | solution.py:83
  206.5 13.6 %collective-permute-start.50 = (bf16[2,1,1,2,64,1152]{5,4,3,2,1,0:T(8,128)(2,1)S(1)}, bf16[2,1,1,2,64,1152]{5,4,3,2,1,0:T(8,128)(2,1)S(1)}, u32[]{:S(2)}, u32[]{:S(2)}) collective-permute-start(bf16[2,1,1,2,64,1152]{5,4,3,2,1,0:T(8,128)(2,1)S(1)} %get-tuple-element.370), channel_id=1, source_target_pairs={{0,96},{96,0},{32,64},{64,32},{1,97},{97,1},{33,65},{65,33},{2,98}... | collective-permute-start | bytes 1769480 | tf_op jit(solution)/shard_map/ppermute | solution.py:83
  208.5 13.3 %collective-permute-start.51 = (bf16[2,2,1,1,64,1152]{5,4,3,2,1,0:T(8,128)(2,1)S(1)}, bf16[2,2,1,1,64,1152]{5,4,3,2,1,0:T(8,128)(2,1)S(1)}, u32[]{:S(2)}, u32[]{:S(2)}) collective-permute-start(bf16[2,2,1,1,64,1152]{5,4,3,2,1,0:T(8,128)(2,1)S(1)} %get-tuple-element.371), channel_id=1, source_target_pairs={{0,24},{24,0},{8,16},{16,8},{1,25},{25,1},{9,17},{17,9},{2,26},{26... | collective-permute-start | bytes 1769480 | tf_op jit(solution)/shard_map/ppermute | solution.py:83
  209.5 12.2 %collective-permute-start.52 = (bf16[1,2,2,1,64,1152]{5,4,3,2,1,0:T(8,128)(2,1)S(1)}, bf16[1,2,2,1,64,1152]{5,4,3,2,1,0:T(8,128)(2,1)S(1)}, u32[]{:S(2)}, u32[]{:S(2)}) collective-permute-start(bf16[1,2,2,1,64,1152]{5,4,3,2,1,0:T(8,128)(2,1)S(1)} %get-tuple-element.372), channel_id=1, source_target_pairs={{0,32},{32,0},{64,96},{96,64},{1,33},{33,1},{65,97},{97,65},{2,34}... | collective-permute-start | bytes 1769480 | tf_op jit(solution)/shard_map/ppermute | solution.py:83
  222.4 15.7 %collective-permute-start.54 = (bf16[1,1,1,2,64,1152]{5,4,3,2,1,0:T(8,128)(2,1)S(1)}, bf16[1,1,1,2,64,1152]{5,4,3,2,1,0:T(8,128)(2,1)S(1)}, u32[]{:S(2)}, u32[]{:S(2)}) collective-permute-start(bf16[1,1,1,2,64,1152]{5,4,3,2,1,0:T(8,128)(2,1)S(1)} %get-tuple-element.386), channel_id=1, source_target_pairs={{0,96},{96,0},{32,64},{64,32},{1,97},{97,1},{33,65},{65,33},{2,98}... | collective-permute-start | bytes 884744 | tf_op jit(solution)/shard_map/ppermute | solution.py:83
  223.7 16.4 %collective-permute-start.55 = (bf16[2,1,1,1,64,1152]{5,4,3,2,1,0:T(8,128)(2,1)S(1)}, bf16[2,1,1,1,64,1152]{5,4,3,2,1,0:T(8,128)(2,1)S(1)}, u32[]{:S(2)}, u32[]{:S(2)}) collective-permute-start(bf16[2,1,1,1,64,1152]{5,4,3,2,1,0:T(8,128)(2,1)S(1)} %get-tuple-element.387), channel_id=1, source_target_pairs={{0,24},{24,0},{8,16},{16,8},{1,25},{25,1},{9,17},{17,9},{2,26},{26... | collective-permute-start | bytes 884744 | tf_op jit(solution)/shard_map/ppermute | solution.py:83
  225.1 15.8 %collective-permute-start.56 = (bf16[1,2,1,1,64,1152]{5,4,3,2,1,0:T(8,128)(2,1)S(1)}, bf16[1,2,1,1,64,1152]{5,4,3,2,1,0:T(8,128)(2,1)S(1)}, u32[]{:S(2)}, u32[]{:S(2)}) collective-permute-start(bf16[1,2,1,1,64,1152]{5,4,3,2,1,0:T(8,128)(2,1)S(1)} %get-tuple-element.388), channel_id=1, source_target_pairs={{0,32},{32,0},{64,96},{96,64},{1,33},{33,1},{65,97},{97,65},{2,34}... | collective-permute-start | bytes 884744 | tf_op jit(solution)/shard_map/ppermute | solution.py:83
  225.1 15.8 %collective-permute-start.57 = (bf16[1,1,2,1,64,1152]{5,4,3,2,1,0:T(8,128)(2,1)S(1)}, bf16[1,1,2,1,64,1152]{5,4,3,2,1,0:T(8,128)(2,1)S(1)}, u32[]{:S(2)}, u32[]{:S(2)}) collective-permute-start(bf16[1,1,2,1,64,1152]{5,4,3,2,1,0:T(8,128)(2,1)S(1)} %get-tuple-element.389), channel_id=1, source_target_pairs={{0,8},{8,0},{16,24},{24,16},{1,9},{9,1},{17,25},{25,17},{2,10},{10... | collective-permute-start | bytes 884744 | tf_op jit(solution)/shard_map/ppermute | solution.py:83
  232.6 22.4 %collective-permute-start.60 = (bf16[2,2,2,1,64,768]{5,4,3,2,1,0:T(8,128)(2,1)S(1)}, bf16[2,2,2,1,64,768]{5,4,3,2,1,0:T(8,128)(2,1)S(1)}, u32[]{:S(2)}, u32[]{:S(2)}) collective-permute-start(bf16[2,2,2,1,64,768]{5,4,3,2,1,0:T(8,128)(2,1)S(1)} %bitcast.151), channel_id=1, source_target_pairs={{0,24},{24,0},{8,16},{16,8},{1,25},{25,1},{9,17},{17,9},{2,26},{26... | collective-permute-start | bytes 2359304 | tf_op jit(solution)/shard_map/ppermute | solution.py:83
  238.1 16.9 %collective-permute-start.59 = (bf16[2,2,1,2,64,768]{5,4,3,2,1,0:T(8,128)(2,1)S(1)}, bf16[2,2,1,2,64,768]{5,4,3,2,1,0:T(8,128)(2,1)S(1)}, u32[]{:S(2)}, u32[]{:S(2)}) collective-permute-start(bf16[2,2,1,2,64,768]{5,4,3,2,1,0:T(8,128)(2,1)S(1)} %bitcast.152), channel_id=1, source_target_pairs={{0,96},{96,0},{32,64},{64,32},{1,97},{97,1},{33,65},{65,33},{2,98}... | collective-permute-start | bytes 2359304 | tf_op jit(solution)/shard_map/ppermute | solution.py:83
  240.1 14.9 %collective-permute-start.53 = (bf16[1,2,2,2,64,768]{5,4,3,2,1,0:T(8,128)(2,1)S(1)}, bf16[1,2,2,2,64,768]{5,4,3,2,1,0:T(8,128)(2,1)S(1)}, u32[]{:S(2)}, u32[]{:S(2)}) collective-permute-start(bf16[1,2,2,2,64,768]{5,4,3,2,1,0:T(8,128)(2,1)S(1)} %bitcast.149), channel_id=1, source_target_pairs={{0,32},{32,0},{64,96},{96,64},{1,33},{33,1},{65,97},{97,65},{2,34}... | collective-permute-start | bytes 2359304 | tf_op jit(solution)/shard_map/ppermute | solution.py:83
  246.8 19.2 %collective-permute-start.58 = (bf16[2,1,2,2,64,768]{5,4,3,2,1,0:T(8,128)(2,1)S(1)}, bf16[2,1,2,2,64,768]{5,4,3,2,1,0:T(8,128)(2,1)S(1)}, u32[]{:S(2)}, u32[]{:S(2)}) collective-permute-start(bf16[2,1,2,2,64,768]{5,4,3,2,1,0:T(8,128)(2,1)S(1)} %bitcast.150), channel_id=1, source_target_pairs={{0,8},{8,0},{16,24},{24,16},{1,9},{9,1},{17,25},{25,17},{2,10},{10... | collective-permute-start | bytes 2359304 | tf_op jit(solution)/shard_map/ppermute | solution.py:83
  359.0 18.6 %collective-permute-start.99 = (bf16[2,2,2,1,64,896]{5,4,3,2,1,0:T(8,128)(2,1)S(1)}, bf16[2,2,2,1,64,896]{5,4,3,2,1,0:T(8,128)(2,1)S(1)}, u32[]{:S(2)}, u32[]{:S(2)}) collective-permute-start(bf16[2,2,2,1,64,896]{5,4,3,2,1,0:T(8,128)(2,1)S(1)} %pad_maximum_fusion.8.refs_0_), channel_id=1, source_target_pairs={{0,24},{24,0},{8,16},{16,8},{1,25},{25,1},{9,17},{17,9},{2,26},{26... | collective-permute-start | bytes 2752520 | tf_op jit(solution)/shard_map/ppermute | solution.py:58
  360.3 14.1 %collective-permute-start.100 = (bf16[1,2,2,2,64,768]{5,4,3,2,1,0:T(8,128)(2,1)S(1)}, bf16[1,2,2,2,64,768]{5,4,3,2,1,0:T(8,128)(2,1)S(1)}, u32[]{:S(2)}, u32[]{:S(2)}) collective-permute-start(bf16[1,2,2,2,64,768]{5,4,3,2,1,0:T(8,128)(2,1)S(1)} %pad_maximum_fusion.16.refs_2_), channel_id=1, source_target_pairs={{0,32},{32,0},{64,96},{96,64},{1,33},{33,1},{65,97},{97,65},{2,34}... | collective-permute-start | bytes 2359304 | tf_op jit(solution)/shard_map/ppermute | solution.py:58
  361.7 13.7 %collective-permute-start.101 = (bf16[2,1,2,2,64,768]{5,4,3,2,1,0:T(8,128)(2,1)S(1)}, bf16[2,1,2,2,64,768]{5,4,3,2,1,0:T(8,128)(2,1)S(1)}, u32[]{:S(2)}, u32[]{:S(2)}) collective-permute-start(bf16[2,1,2,2,64,768]{5,4,3,2,1,0:T(8,128)(2,1)S(1)} %pad_maximum_fusion.17.refs_4_), channel_id=1, source_target_pairs={{0,8},{8,0},{16,24},{24,16},{1,9},{9,1},{17,25},{25,17},{2,10},{10... | collective-permute-start | bytes 2359304 | tf_op jit(solution)/shard_map/ppermute | solution.py:58
  361.7 14.7 %collective-permute-start.102 = (bf16[2,2,1,2,64,768]{5,4,3,2,1,0:T(8,128)(2,1)S(1)}, bf16[2,2,1,2,64,768]{5,4,3,2,1,0:T(8,128)(2,1)S(1)}, u32[]{:S(2)}, u32[]{:S(2)}) collective-permute-start(bf16[2,2,1,2,64,768]{5,4,3,2,1,0:T(8,128)(2,1)S(1)} %pad_maximum_fusion.18.refs_6_), channel_id=1, source_target_pairs={{0,96},{96,0},{32,64},{64,32},{1,97},{97,1},{33,65},{65,33},{2,98}... | collective-permute-start | bytes 2359304 | tf_op jit(solution)/shard_map/ppermute | solution.py:58
  (121 other events, 1252.6 us)

commit v2 on v1

--- a/solution.py
+++ b/solution.py
@@ -883,7 +883,9 @@
         held = together(gather_step(held, step))
     fresh = gather_came(held, 3)
     pieces = [x for pair in zip(held, fresh) for x in pair]
-    gain_parts = jnp.concatenate([x[..., FF // 4 :] for x in pieces[:2]], axis=3)
+    gain_parts = [x[..., FF // 4 :] for x in pieces[:2]]
+    *gain_parts, iterate = together([*gain_parts, iterate_rows(pieces)])
+    gain_parts = jnp.concatenate(gain_parts, axis=3)
     gain_parts = gain_parts.reshape(16, 64 * HD)
     place = lax.broadcasted_iota(jnp.int32, (16, 16), 1)
     of_z = jnp.bitwise_xor(z, jnp.bitwise_xor(place // 8, (place // 2) % 2 * 3))
@@ -891,7 +893,6 @@
     in_turn = (lax.broadcasted_iota(jnp.int32, (16, 16), 0) == of_z * 4 + of_y).astype(LOW)
     gain_parts = dot(in_turn, gain_parts)[:, : 3 * gain_sum.shape[0]].reshape(16, 3, -1)
     gain_grad = jnp.sum(gain_parts[:, 0] + gain_parts[:, 1] + gain_parts[:, 2], axis=0)
-    iterate = iterate_rows(pieces)
     kept = core_pick(iterate[:32], iterate[32:])
     got = swap(core_pick(iterate[32:], iterate[:32]))
     iterate = jnp.stack([core_pick(kept, got), core_pick(got, kept)]).astype(F32)

time: 452 us -> 441 us (0.976)
  local copies, waits for them, and re-layouts: 15.6 us -> 5.63 us
    unnamed x102 -> x116, local copies, waits for them, and re-layouts: 13.6 us -> 4.44 us
  transfers between devices with their start and end apart: 104 -> 104, of which waited for: 59 -> 60; matrix products, arithmetic and copies ran while one was open for 6% -> 6% of each run, Pallas kernels for 12% -> 12%
where the time goes in v2:
time: 441 us; the launch traced here: 433 us
  starting transfers between devices  142 us (32%)
  waiting for transfers between devices  134 us (30%)
  Pallas kernels  116 us (26%)
  other arithmetic  18.1 us (4%)
  matrix products  14.2 us (3%)
  local copies, waits for them, and re-layouts  5.63 us (1%)
    ppermute x48, waiting for transfers between devices, gather_came(): fresh.append(lax.ppermute(quarters[i], axis, pairs))  61.9 us
    ppermute x14, starting transfers between devices, swap(): return lax.ppermute(x, 'dp_2', ((0, 1), (1, 0)))  54.4 us
    ppermute x48, starting transfers between devices, gather_came(): fresh.append(lax.ppermute(quarters[i], axis, pairs))  45.8 us
    pallas_call x1, Pallas kernels, iterate_rows(): pl.pallas_call(iterate_kernel, in_specs=[pl.BlockSpec(memory_space=pl.ANY...  45.5 us
    ppermute x32, waiting for transfers between devices, scatter_step(): came.append(lax.ppermute(sent[i], axis, pairs))  40.9 us
    ppermute x32, starting transfers between devices, scatter_step(): came.append(lax.ppermute(sent[i], axis, pairs))  28.7 us
    pallas_call x4, Pallas kernels, heads_backward(): pl.pallas_call(functools.partial(heads_back_kernel, link), grid=(tokens /...  21.4 us
    pallas_call x8, Pallas kernels, terms(): pl.pallas_call(functools.partial(terms_kernel, link), grid=(4,), in_specs...  19.2 us
  transfers between devices with their start and end apart: 104, of which 60 were waited for; matrix products, arithmetic and copies ran while one was open for 6% of the time, Pallas kernels for 12%

profile of v2, /device:TPU:1, one launch (start us, length us, event | category | flops | bytes accessed | tf_op | source)
XLA Modules:
  0.0 432.6 jit_solution(14684559246960077959)
XLA Ops:
  12.9 6.7 %collective-permute-done.3 = bf16[1,2,2,16,3072]{4,3,2,1,0:T(8,128)(2,1)S(1)} collective-permute-done((bf16[1,2,2,16,3072]{4,3,2,1,0:T(8,128)(2,1)S(1)}, bf16[1,2,2,16,3072]{4,3,2,1,0:T(8,128)(2,1)S(1)}, u32[]{:S(2)}, u32[]{:S(2)}) %collective-permute-start.3) | collective-permute-done | bytes 393248 | tf_op jit(solution)/shard_map/ppermute | solution.py:103
  21.7 2.9 collective-permute-start.4
  40.7 2.7 collective-permute-start.11
  52.0 3.7 collective-permute-done.21
  58.9 8.5 %collective-permute-done.17 = bf16[2,2,1,1,64,768]{5,4,3,2,1,0:T(8,128)(2,1)S(1)} collective-permute-done((bf16[2,2,1,1,64,768]{5,4,3,2,1,0:T(8,128)(2,1)S(1)}, bf16[2,2,1,1,64,768]{5,4,3,2,1,0:T(8,128)(2,1)S(1)}, u32[]{:S(2)}, u32[]{:S(2)}) %collective-permute-start.17) | collective-permute-done | bytes 393248 | tf_op jit(solution)/shard_map/ppermute | solution.py:58
  73.9 4.2 collective-permute-done.29
  83.4 13.0 %collective-permute-done.25.fresh_ref = bf16[2,2,2,1,64,768]{5,4,3,2,1,0:T(8,128)(2,1)S(1)} collective-permute-done((bf16[2,2,2,1,64,768]{5,4,3,2,1,0:T(8,128)(2,1)S(1)}, bf16[2,2,2,1,64,768]{5,4,3,2,1,0:T(8,128)(2,1)S(1)}, u32[]{:S(2)}, u32[]{:S(2)}) %collective-permute-start.25) | collective-permute-done | bytes 786464 | tf_op jit(solution)/shard_map/ppermute | solution.py:58
  103.2 20.6 %collective-permute-start.37 = (bf16[256,1024]{1,0:T(8,128)(2,1)S(1)}, bf16[256,1024]{1,0:T(8,128)(2,1)S(1)}, u32[]{:S(2)}, u32[]{:S(2)}) collective-permute-start(bf16[256,1024]{1,0:T(8,128)(2,1)S(1)} %multiply_convert_fusion.2), channel_id=1, source_target_pairs={{0,4},{4,0},{1,5},{5,1},{2,6},{6,2},{3,7},{7,3},{8,12},{12,8},{9,1... | collective-permute-start | bytes 1572872 | tf_op jit(solution)/shard_map/ppermute | solution.py:47
  125.7 3.0 shard_map.171
  129.8 2.9 shard_map.172
  132.7 3.0 shard_map.173
  136.7 3.0 shard_map.174
  145.4 16.0 %shard_map.175 = (bf16[512,1536]{1,0:T(8,128)(2,1)S(1)}, bf16[512,3072]{1,0:T(8,128)(2,1)}, f32[256,1024]{1,0:T(8,128)S(1)}, bf16[256,1024]{1,0:T(8,128)(2,1)S(1...) custom-call(bf16[512,1024]{1,0:T(8,128)(2,1)S(1)} %pad_maximum_fusion.5.input_ref.first_left, ...), custom_call_target="tpu_custom_call" | custom-call | flops 1048576 | bytes 65536 | tf_op jit(solution)/shard_map/pallas_call | solution.py:511
  171.7 2.8 shard_map.178
  175.5 2.8 shard_map.177
  182.5 5.4 %shard_map.176 = (bf16[512,512]{1,0:T(8,128)(2,1)S(1)}, f32[16,128]{1,0:T(8,128)S(1)}, f32[512,1024]{1,0:T(8,128)S(1)}) custom-call(f32[512,512]{1,0:T(8,128)S(1)} %copy-done.10, bf16[512,1024]{1,0:T(8,128)(2,1)S(1)} %pad_maximum_fusion.7.branch_ref.second_left, bf16[2,2,2,1,64,768]{5,4,3,2,1,0:T(8,128)(2,1)S(1)} %pad_maximum_fusion.11.held_ref, ...), custom_call_target="tpu_custom_call" | custom-call | flops 1048576 | bytes 65536 | tf_op jit(solution)/shard_map/pallas_call | solution.py:440
  187.9 5.4 %shard_map.181 = (bf16[512,512]{1,0:T(8,128)(2,1)S(1)}, f32[16,128]{1,0:T(8,128)S(1)}, f32[512,1024]{1,0:T(8,128)S(1)}) custom-call(f32[512,512]{1,0:T(8,128)S(1)} %copy-done.8, bf16[512,1024]{1,0:T(8,128)(2,1)S(1)} %pad_maximum_fusion.7.branch_ref.second_left, bf16[1,2,2,2,64,768]{5,4,3,2,1,0:T(8,128)(2,1)S(1)} %pad_maximum_fusion.12.held_ref, ...), custom_call_target="tpu_custom_call" | custom-call | flops 1048576 | bytes 65536 | tf_op jit(solution)/shard_map/pallas_call | solution.py:440
  194.9 4.1 collective-permute-done.47
  201.1 3.5 collective-permute-done.45
  209.7 5.3 %shard_map.183 = (bf16[512,512]{1,0:T(8,128)(2,1)S(1)}, f32[16,128]{1,0:T(8,128)S(1)}, f32[512,1024]{1,0:T(8,128)S(1)}) custom-call(f32[512,512]{1,0:T(8,128)S(1)} %copy-done.6, bf16[512,1024]{1,0:T(8,128)(2,1)S(1)} %pad_maximum_fusion.7.branch_ref.second_left, bf16[2,1,2,2,64,768]{5,4,3,2,1,0:T(8,128)(2,1)S(1)} %pad_maximum_fusion.13.held_ref, ...), custom_call_target="tpu_custom_call" | custom-call | flops 1048576 | bytes 65536 | tf_op jit(solution)/shard_map/pallas_call | solution.py:440
  225.0 5.4 %shard_map.185 = (bf16[512,512]{1,0:T(8,128)(2,1)S(1)}, f32[16,128]{1,0:T(8,128)S(1)}, f32[512,1024]{1,0:T(8,128)S(1)}) custom-call(f32[512,512]{1,0:T(8,128)S(1)} %copy-done.4, bf16[512,1024]{1,0:T(8,128)(2,1)S(1)} %pad_maximum_fusion.7.branch_ref.second_left, bf16[2,2,1,2,64,768]{5,4,3,2,1,0:T(8,128)(2,1)S(1)} %pad_maximum_fusion.14.held_ref, ...), custom_call_target="tpu_custom_call" | custom-call | flops 1048576 | bytes 65536 | tf_op jit(solution)/shard_map/pallas_call | solution.py:440
  241.5 5.4 %collective-permute-start.61 = (bf16[256,1024]{1,0:T(8,128)(2,1)S(1)}, bf16[256,1024]{1,0:T(8,128)(2,1)S(1)}, u32[]{:S(2)}, u32[]{:S(2)}) collective-permute-start(bf16[256,1024]{1,0:T(8,128)(2,1)S(1)} %slice.771), channel_id=1, source_target_pairs={{0,4},{4,0},{1,5},{5,1},{2,6},{6,2},{3,7},{7,3},{8,12},{12,8},{9,1... | collective-permute-start | bytes 1572872 | tf_op jit(solution)/shard_map/ppermute | solution.py:47
  255.2 11.0 %collective-permute-done.58 = bf16[2,1,2,2,64,768]{5,4,3,2,1,0:T(8,128)(2,1)S(1)} collective-permute-done((bf16[2,1,2,2,64,768]{5,4,3,2,1,0:T(8,128)(2,1)S(1)}, bf16[2,1,2,2,64,768]{5,4,3,2,1,0:T(8,128)(2,1)S(1)}, u32[]{:S(2)}, u32[]{:S(2)}) %collective-permute-start.58) | collective-permute-done | bytes 786464 | tf_op jit(solution)/shard_map/ppermute | solution.py:83
  272.8 4.1 collective-permute-done.62
  300.2 6.3 %collective-permute-start.81 = (bf16[32,7680]{1,0:T(8,128)(2,1)S(1)}, bf16[32,7680]{1,0:T(8,128)(2,1)S(1)}, u32[]{:S(2)}, u32[]{:S(2)}) collective-permute-start(bf16[32,7680]{1,0:T(8,128)(2,1)S(1)} %get-tuple-element.565), channel_id=1, source_target_pairs={{0,4},{4,0},{1,5},{5,1},{2,6},{6,2},{3,7},{7,3},{8,12},{12,8},{9,1... | collective-permute-start | bytes 1474568 | tf_op jit(solution)/shard_map/ppermute | solution.py:47
  312.1 7.1 %collective-permute-done.82 = bf16[4,16,3072]{2,1,0:T(8,128)(2,1)S(1)} collective-permute-done((bf16[4,16,3072]{2,1,0:T(8,128)(2,1)S(1)}, bf16[4,16,3072]{2,1,0:T(8,128)(2,1)S(1)}, u32[]{:S(2)}, u32[]{:S(2)}) %collective-permute-start.82) | collective-permute-done | bytes 393248 | tf_op jit(solution)/shard_map/ppermute | solution.py:854
  323.6 4.1 collective-permute-done.84
  329.8 2.7 collective-permute-start.86
  351.6 4.7 %collective-permute-start.42 = (bf16[256,1024]{1,0:T(8,128)(2,1)S(1)}, bf16[256,1024]{1,0:T(8,128)(2,1)S(1)}, u32[]{:S(2)}, u32[]{:S(2)}) collective-permute-start(bf16[256,1024]{1,0:T(8,128)(2,1)S(1)} %copy-done.18), channel_id=1, source_target_pairs={{0,4},{4,0},{1,5},{5,1},{2,6},{6,2},{3,7},{7,3},{8,12},{12,8},{9,1... | collective-permute-start | bytes 1572872 | tf_op jit(solution)/shard_map/ppermute | solution.py:47
  365.6 9.1 %collective-permute-done.100.refs_3_ = bf16[1,2,2,2,64,768]{5,4,3,2,1,0:T(8,128)(2,1)S(1)} collective-permute-done((bf16[1,2,2,2,64,768]{5,4,3,2,1,0:T(8,128)(2,1)S(1)}, bf16[1,2,2,2,64,768]{5,4,3,2,1,0:T(8,128)(2,1)S(1)}, u32[]{:S(2)}, u32[]{:S(2)}) %collective-permute-start.100) | collective-permute-done | bytes 786464 | tf_op jit(solution)/shard_map/ppermute | solution.py:58
  377.9 45.5 %shard_map.189 = bf16[64,3072]{1,0:T(8,128)(2,1)S(1)} custom-call(bf16[2,2,2,1,64,896]{5,4,3,2,1,0:T(8,128)(2,1)S(1)} %pad_maximum_fusion.8.refs_0_, bf16[2,2,2,1,64,896]{5,4,3,2,1,0:T(8,128)(2,1)S(1)} %collective-permute-done.99.refs_1_, bf16[1,2,2,2,64,768]{5,4,3,2,1,0:T(8,128)(2,1)S(1)} %pad_maximum_fusion.16.refs_2_, ...), custom_call_target="tpu_custom_call" | custom-call | flops 49999998976 | bytes 8388608 | tf_op jit(solution)/shard_map/pallas_call | solution.py:376
  424.5 5.4 %collective-permute-start.103 = (bf16[32,3072]{1,0:T(8,128)(2,1)S(1)}, bf16[32,3072]{1,0:T(8,128)(2,1)S(1)}, u32[]{:S(2)}, u32[]{:S(2)}) collective-permute-start(bf16[32,3072]{1,0:T(8,128)(2,1)S(1)} %broadcast_select_fusion.2), channel_id=1, source_target_pairs={{0,4},{4,0},{1,5},{5,1},{2,6},{6,2},{3,7},{7,3},{8,12},{12,8},{9,1... | collective-permute-start | bytes 589832 | tf_op jit(solution)/shard_map/ppermute | solution.py:47
  (489 shorter events, 199.3 us)
Async XLA Ops:
  5.9 97.4 %collective-permute-start.38 = (s32[2,128]{1,0:T(2,128)}, s32[2,128]{1,0:T(2,128)S(1)}, u32[]{:S(2)}, u32[]{:S(2)}) collective-permute-start(s32[2,128]{1,0:T(2,128)} %param.14), channel_id=1, source_target_pairs={{0,4},{4,0},{1,5},{5,1},{2,6},{6,2},{3,7},{7,3},{8,12},{12,8},{9,1... | collective-permute-start | bytes 3080 | tf_op jit(solution)/shard_map/ppermute | solution.py:47
  78.1 18.3 %collective-permute-start.25 = (bf16[2,2,2,1,64,768]{5,4,3,2,1,0:T(8,128)(2,1)S(1)}, bf16[2,2,2,1,64,768]{5,4,3,2,1,0:T(8,128)(2,1)S(1)}, u32[]{:S(2)}, u32[]{:S(2)}) collective-permute-start(bf16[2,2,2,1,64,768]{5,4,3,2,1,0:T(8,128)(2,1)S(1)} %pad_maximum_fusion.11.held_ref), channel_id=1, source_target_pairs={{0,24},{24,0},{8,16},{16,8},{1,25},{25,1},{9,17},{17,9},{2,26},{26... | collective-permute-start | bytes 2359304 | tf_op jit(solution)/shard_map/ppermute | solution.py:58
  80.5 16.2 %collective-permute-start.26 = (bf16[1,2,2,2,64,768]{5,4,3,2,1,0:T(8,128)(2,1)S(1)}, bf16[1,2,2,2,64,768]{5,4,3,2,1,0:T(8,128)(2,1)S(1)}, u32[]{:S(2)}, u32[]{:S(2)}) collective-permute-start(bf16[1,2,2,2,64,768]{5,4,3,2,1,0:T(8,128)(2,1)S(1)} %pad_maximum_fusion.12.held_ref), channel_id=1, source_target_pairs={{0,32},{32,0},{64,96},{96,64},{1,33},{33,1},{65,97},{97,65},{2,34}... | collective-permute-start | bytes 2359304 | tf_op jit(solution)/shard_map/ppermute | solution.py:58
  81.1 17.2 %collective-permute-start.27 = (bf16[2,1,2,2,64,768]{5,4,3,2,1,0:T(8,128)(2,1)S(1)}, bf16[2,1,2,2,64,768]{5,4,3,2,1,0:T(8,128)(2,1)S(1)}, u32[]{:S(2)}, u32[]{:S(2)}) collective-permute-start(bf16[2,1,2,2,64,768]{5,4,3,2,1,0:T(8,128)(2,1)S(1)} %pad_maximum_fusion.13.held_ref), channel_id=1, source_target_pairs={{0,8},{8,0},{16,24},{24,16},{1,9},{9,1},{17,25},{25,17},{2,10},{10... | collective-permute-start | bytes 2359304 | tf_op jit(solution)/shard_map/ppermute | solution.py:58
  82.1 16.1 %collective-permute-start.28 = (bf16[2,2,1,2,64,768]{5,4,3,2,1,0:T(8,128)(2,1)S(1)}, bf16[2,2,1,2,64,768]{5,4,3,2,1,0:T(8,128)(2,1)S(1)}, u32[]{:S(2)}, u32[]{:S(2)}) collective-permute-start(bf16[2,2,1,2,64,768]{5,4,3,2,1,0:T(8,128)(2,1)S(1)} %pad_maximum_fusion.14.held_ref), channel_id=1, source_target_pairs={{0,96},{96,0},{32,64},{64,32},{1,97},{97,1},{33,65},{65,33},{2,98}... | collective-permute-start | bytes 2359304 | tf_op jit(solution)/shard_map/ppermute | solution.py:58
  98.3 41.4 %collective-permute-start.33 = (bf16[2,2,2,1,64,1152]{5,4,3,2,1,0:T(8,128)(2,1)S(1)}, bf16[2,2,2,1,64,1152]{5,4,3,2,1,0:T(8,128)(2,1)S(1)}, u32[]{:S(2)}, u32[]{:S(2)}) collective-permute-start(bf16[2,2,2,1,64,1152]{5,4,3,2,1,0:T(8,128)(2,1)S(1)} %pad_maximum_fusion.refs_0_), channel_id=1, source_target_pairs={{0,24},{24,0},{8,16},{16,8},{1,25},{25,1},{9,17},{17,9},{2,26},{26... | collective-permute-start | bytes 3538952 | tf_op jit(solution)/shard_map/ppermute | solution.py:58
  100.4 39.3 %collective-permute-start.34 = (bf16[1,2,2,2,64,1152]{5,4,3,2,1,0:T(8,128)(2,1)S(1)}, bf16[1,2,2,2,64,1152]{5,4,3,2,1,0:T(8,128)(2,1)S(1)}, u32[]{:S(2)}, u32[]{:S(2)}) collective-permute-start(bf16[1,2,2,2,64,1152]{5,4,3,2,1,0:T(8,128)(2,1)S(1)} %pad_maximum_fusion.1.refs_2_), channel_id=1, source_target_pairs={{0,32},{32,0},{64,96},{96,64},{1,33},{33,1},{65,97},{97,65},{2,34}... | collective-permute-start | bytes 3538952 | tf_op jit(solution)/shard_map/ppermute | solution.py:58
  101.1 38.6 %collective-permute-start.35 = (bf16[2,1,2,2,64,1152]{5,4,3,2,1,0:T(8,128)(2,1)S(1)}, bf16[2,1,2,2,64,1152]{5,4,3,2,1,0:T(8,128)(2,1)S(1)}, u32[]{:S(2)}, u32[]{:S(2)}) collective-permute-start(bf16[2,1,2,2,64,1152]{5,4,3,2,1,0:T(8,128)(2,1)S(1)} %pad_maximum_fusion.2.refs_4_), channel_id=1, source_target_pairs={{0,8},{8,0},{16,24},{24,16},{1,9},{9,1},{17,25},{25,17},{2,10},{10... | collective-permute-start | bytes 3538952 | tf_op jit(solution)/shard_map/ppermute | solution.py:58
  101.1 38.6 %collective-permute-start.36 = (bf16[2,2,1,2,64,1152]{5,4,3,2,1,0:T(8,128)(2,1)S(1)}, bf16[2,2,1,2,64,1152]{5,4,3,2,1,0:T(8,128)(2,1)S(1)}, u32[]{:S(2)}, u32[]{:S(2)}) collective-permute-start(bf16[2,2,1,2,64,1152]{5,4,3,2,1,0:T(8,128)(2,1)S(1)} %pad_maximum_fusion.3.refs_6_), channel_id=1, source_target_pairs={{0,96},{96,0},{32,64},{64,32},{1,97},{97,1},{33,65},{65,33},{2,98}... | collective-permute-start | bytes 3538952 | tf_op jit(solution)/shard_map/ppermute | solution.py:58
  103.2 22.2 %collective-permute-start.37 = (bf16[256,1024]{1,0:T(8,128)(2,1)S(1)}, bf16[256,1024]{1,0:T(8,128)(2,1)S(1)}, u32[]{:S(2)}, u32[]{:S(2)}) collective-permute-start(bf16[256,1024]{1,0:T(8,128)(2,1)S(1)} %multiply_convert_fusion.2), channel_id=1, source_target_pairs={{0,4},{4,0},{1,5},{5,1},{2,6},{6,2},{3,7},{7,3},{8,12},{12,8},{9,1... | collective-permute-start | bytes 1572872 | tf_op jit(solution)/shard_map/ppermute | solution.py:47
  161.5 17.0 %collective-permute-start.43 = (bf16[256,1024]{1,0:T(8,128)(2,1)S(1)}, bf16[256,1024]{1,0:T(8,128)(2,1)S(1)}, u32[]{:S(2)}, u32[]{:S(2)}) collective-permute-start(bf16[256,1024]{1,0:T(8,128)(2,1)S(1)} %get-tuple-element.349), channel_id=1, source_target_pairs={{0,4},{4,0},{1,5},{5,1},{2,6},{6,2},{3,7},{7,3},{8,12},{12,8},{9,1... | collective-permute-start | bytes 1572872 | tf_op jit(solution)/shard_map/ppermute | solution.py:47
  166.5 28.4 %collective-permute-start.48 = (bf16[2,2,2,1,64,1152]{5,4,3,2,1,0:T(8,128)(2,1)S(1)}, bf16[2,2,2,1,64,1152]{5,4,3,2,1,0:T(8,128)(2,1)S(1)}, u32[]{:S(2)}, u32[]{:S(2)}) collective-permute-start(bf16[2,2,2,1,64,1152]{5,4,3,2,1,0:T(8,128)(2,1)S(1)} %bitcast.145), channel_id=1, source_target_pairs={{0,24},{24,0},{8,16},{16,8},{1,25},{25,1},{9,17},{17,9},{2,26},{26... | collective-permute-start | bytes 3538952 | tf_op jit(solution)/shard_map/ppermute | solution.py:83
  170.8 28.3 %collective-permute-start.47 = (bf16[2,2,1,2,64,1152]{5,4,3,2,1,0:T(8,128)(2,1)S(1)}, bf16[2,2,1,2,64,1152]{5,4,3,2,1,0:T(8,128)(2,1)S(1)}, u32[]{:S(2)}, u32[]{:S(2)}) collective-permute-start(bf16[2,2,1,2,64,1152]{5,4,3,2,1,0:T(8,128)(2,1)S(1)} %bitcast.146), channel_id=1, source_target_pairs={{0,96},{96,0},{32,64},{64,32},{1,97},{97,1},{33,65},{65,33},{2,98}... | collective-permute-start | bytes 3538952 | tf_op jit(solution)/shard_map/ppermute | solution.py:83
  174.5 26.6 %collective-permute-start.46 = (bf16[2,1,2,2,64,1152]{5,4,3,2,1,0:T(8,128)(2,1)S(1)}, bf16[2,1,2,2,64,1152]{5,4,3,2,1,0:T(8,128)(2,1)S(1)}, u32[]{:S(2)}, u32[]{:S(2)}) collective-permute-start(bf16[2,1,2,2,64,1152]{5,4,3,2,1,0:T(8,128)(2,1)S(1)} %bitcast.147), channel_id=1, source_target_pairs={{0,8},{8,0},{16,24},{24,16},{1,9},{9,1},{17,25},{25,17},{2,10},{10... | collective-permute-start | bytes 3538952 | tf_op jit(solution)/shard_map/ppermute | solution.py:83
  178.3 26.3 %collective-permute-start.45 = (bf16[1,2,2,2,64,1152]{5,4,3,2,1,0:T(8,128)(2,1)S(1)}, bf16[1,2,2,2,64,1152]{5,4,3,2,1,0:T(8,128)(2,1)S(1)}, u32[]{:S(2)}, u32[]{:S(2)}) collective-permute-start(bf16[1,2,2,2,64,1152]{5,4,3,2,1,0:T(8,128)(2,1)S(1)} %bitcast.148), channel_id=1, source_target_pairs={{0,32},{32,0},{64,96},{96,64},{1,33},{33,1},{65,97},{97,65},{2,34}... | collective-permute-start | bytes 3538952 | tf_op jit(solution)/shard_map/ppermute | solution.py:83
  205.9 12.8 %collective-permute-start.49 = (bf16[1,1,2,2,64,1152]{5,4,3,2,1,0:T(8,128)(2,1)S(1)}, bf16[1,1,2,2,64,1152]{5,4,3,2,1,0:T(8,128)(2,1)S(1)}, u32[]{:S(2)}, u32[]{:S(2)}) collective-permute-start(bf16[1,1,2,2,64,1152]{5,4,3,2,1,0:T(8,128)(2,1)S(1)} %get-tuple-element.372), channel_id=1, source_target_pairs={{0,8},{8,0},{16,24},{24,16},{1,9},{9,1},{17,25},{25,17},{2,10},{10... | collective-permute-start | bytes 1769480 | tf_op jit(solution)/shard_map/ppermute | solution.py:83
  206.5 13.6 %collective-permute-start.50 = (bf16[2,1,1,2,64,1152]{5,4,3,2,1,0:T(8,128)(2,1)S(1)}, bf16[2,1,1,2,64,1152]{5,4,3,2,1,0:T(8,128)(2,1)S(1)}, u32[]{:S(2)}, u32[]{:S(2)}) collective-permute-start(bf16[2,1,1,2,64,1152]{5,4,3,2,1,0:T(8,128)(2,1)S(1)} %get-tuple-element.373), channel_id=1, source_target_pairs={{0,96},{96,0},{32,64},{64,32},{1,97},{97,1},{33,65},{65,33},{2,98}... | collective-permute-start | bytes 1769480 | tf_op jit(solution)/shard_map/ppermute | solution.py:83
  208.6 13.3 %collective-permute-start.51 = (bf16[2,2,1,1,64,1152]{5,4,3,2,1,0:T(8,128)(2,1)S(1)}, bf16[2,2,1,1,64,1152]{5,4,3,2,1,0:T(8,128)(2,1)S(1)}, u32[]{:S(2)}, u32[]{:S(2)}) collective-permute-start(bf16[2,2,1,1,64,1152]{5,4,3,2,1,0:T(8,128)(2,1)S(1)} %get-tuple-element.374), channel_id=1, source_target_pairs={{0,24},{24,0},{8,16},{16,8},{1,25},{25,1},{9,17},{17,9},{2,26},{26... | collective-permute-start | bytes 1769480 | tf_op jit(solution)/shard_map/ppermute | solution.py:83
  209.7 12.2 %collective-permute-start.52 = (bf16[1,2,2,1,64,1152]{5,4,3,2,1,0:T(8,128)(2,1)S(1)}, bf16[1,2,2,1,64,1152]{5,4,3,2,1,0:T(8,128)(2,1)S(1)}, u32[]{:S(2)}, u32[]{:S(2)}) collective-permute-start(bf16[1,2,2,1,64,1152]{5,4,3,2,1,0:T(8,128)(2,1)S(1)} %get-tuple-element.375), channel_id=1, source_target_pairs={{0,32},{32,0},{64,96},{96,64},{1,33},{33,1},{65,97},{97,65},{2,34}... | collective-permute-start | bytes 1769480 | tf_op jit(solution)/shard_map/ppermute | solution.py:83
  222.6 15.5 %collective-permute-start.54 = (bf16[1,1,1,2,64,1152]{5,4,3,2,1,0:T(8,128)(2,1)S(1)}, bf16[1,1,1,2,64,1152]{5,4,3,2,1,0:T(8,128)(2,1)S(1)}, u32[]{:S(2)}, u32[]{:S(2)}) collective-permute-start(bf16[1,1,1,2,64,1152]{5,4,3,2,1,0:T(8,128)(2,1)S(1)} %get-tuple-element.389), channel_id=1, source_target_pairs={{0,96},{96,0},{32,64},{64,32},{1,97},{97,1},{33,65},{65,33},{2,98}... | collective-permute-start | bytes 884744 | tf_op jit(solution)/shard_map/ppermute | solution.py:83
  223.7 16.6 %collective-permute-start.55 = (bf16[2,1,1,1,64,1152]{5,4,3,2,1,0:T(8,128)(2,1)S(1)}, bf16[2,1,1,1,64,1152]{5,4,3,2,1,0:T(8,128)(2,1)S(1)}, u32[]{:S(2)}, u32[]{:S(2)}) collective-permute-start(bf16[2,1,1,1,64,1152]{5,4,3,2,1,0:T(8,128)(2,1)S(1)} %get-tuple-element.390), channel_id=1, source_target_pairs={{0,24},{24,0},{8,16},{16,8},{1,25},{25,1},{9,17},{17,9},{2,26},{26... | collective-permute-start | bytes 884744 | tf_op jit(solution)/shard_map/ppermute | solution.py:83
  225.0 16.1 %collective-permute-start.56 = (bf16[1,2,1,1,64,1152]{5,4,3,2,1,0:T(8,128)(2,1)S(1)}, bf16[1,2,1,1,64,1152]{5,4,3,2,1,0:T(8,128)(2,1)S(1)}, u32[]{:S(2)}, u32[]{:S(2)}) collective-permute-start(bf16[1,2,1,1,64,1152]{5,4,3,2,1,0:T(8,128)(2,1)S(1)} %get-tuple-element.391), channel_id=1, source_target_pairs={{0,32},{32,0},{64,96},{96,64},{1,33},{33,1},{65,97},{97,65},{2,34}... | collective-permute-start | bytes 884744 | tf_op jit(solution)/shard_map/ppermute | solution.py:83
  225.0 16.1 %collective-permute-start.57 = (bf16[1,1,2,1,64,1152]{5,4,3,2,1,0:T(8,128)(2,1)S(1)}, bf16[1,1,2,1,64,1152]{5,4,3,2,1,0:T(8,128)(2,1)S(1)}, u32[]{:S(2)}, u32[]{:S(2)}) collective-permute-start(bf16[1,1,2,1,64,1152]{5,4,3,2,1,0:T(8,128)(2,1)S(1)} %get-tuple-element.392), channel_id=1, source_target_pairs={{0,8},{8,0},{16,24},{24,16},{1,9},{9,1},{17,25},{25,17},{2,10},{10... | collective-permute-start | bytes 884744 | tf_op jit(solution)/shard_map/ppermute | solution.py:83
  232.4 22.7 %collective-permute-start.60 = (bf16[2,2,2,1,64,768]{5,4,3,2,1,0:T(8,128)(2,1)S(1)}, bf16[2,2,2,1,64,768]{5,4,3,2,1,0:T(8,128)(2,1)S(1)}, u32[]{:S(2)}, u32[]{:S(2)}) collective-permute-start(bf16[2,2,2,1,64,768]{5,4,3,2,1,0:T(8,128)(2,1)S(1)} %bitcast.151), channel_id=1, source_target_pairs={{0,24},{24,0},{8,16},{16,8},{1,25},{25,1},{9,17},{17,9},{2,26},{26... | collective-permute-start | bytes 2359304 | tf_op jit(solution)/shard_map/ppermute | solution.py:83
  238.1 17.1 %collective-permute-start.59 = (bf16[2,2,1,2,64,768]{5,4,3,2,1,0:T(8,128)(2,1)S(1)}, bf16[2,2,1,2,64,768]{5,4,3,2,1,0:T(8,128)(2,1)S(1)}, u32[]{:S(2)}, u32[]{:S(2)}) collective-permute-start(bf16[2,2,1,2,64,768]{5,4,3,2,1,0:T(8,128)(2,1)S(1)} %bitcast.152), channel_id=1, source_target_pairs={{0,96},{96,0},{32,64},{64,32},{1,97},{97,1},{33,65},{65,33},{2,98}... | collective-permute-start | bytes 2359304 | tf_op jit(solution)/shard_map/ppermute | solution.py:83
  240.2 15.0 %collective-permute-start.53 = (bf16[1,2,2,2,64,768]{5,4,3,2,1,0:T(8,128)(2,1)S(1)}, bf16[1,2,2,2,64,768]{5,4,3,2,1,0:T(8,128)(2,1)S(1)}, u32[]{:S(2)}, u32[]{:S(2)}) collective-permute-start(bf16[1,2,2,2,64,768]{5,4,3,2,1,0:T(8,128)(2,1)S(1)} %bitcast.149), channel_id=1, source_target_pairs={{0,32},{32,0},{64,96},{96,64},{1,33},{33,1},{65,97},{97,65},{2,34}... | collective-permute-start | bytes 2359304 | tf_op jit(solution)/shard_map/ppermute | solution.py:83
  247.0 19.2 %collective-permute-start.58 = (bf16[2,1,2,2,64,768]{5,4,3,2,1,0:T(8,128)(2,1)S(1)}, bf16[2,1,2,2,64,768]{5,4,3,2,1,0:T(8,128)(2,1)S(1)}, u32[]{:S(2)}, u32[]{:S(2)}) collective-permute-start(bf16[2,1,2,2,64,768]{5,4,3,2,1,0:T(8,128)(2,1)S(1)} %bitcast.150), channel_id=1, source_target_pairs={{0,8},{8,0},{16,24},{24,16},{1,9},{9,1},{17,25},{25,17},{2,10},{10... | collective-permute-start | bytes 2359304 | tf_op jit(solution)/shard_map/ppermute | solution.py:83
  351.6 11.8 %collective-permute-start.42 = (bf16[256,1024]{1,0:T(8,128)(2,1)S(1)}, bf16[256,1024]{1,0:T(8,128)(2,1)S(1)}, u32[]{:S(2)}, u32[]{:S(2)}) collective-permute-start(bf16[256,1024]{1,0:T(8,128)(2,1)S(1)} %copy-done.18), channel_id=1, source_target_pairs={{0,4},{4,0},{1,5},{5,1},{2,6},{6,2},{3,7},{7,3},{8,12},{12,8},{9,1... | collective-permute-start | bytes 1572872 | tf_op jit(solution)/shard_map/ppermute | solution.py:47
  359.2 18.7 %collective-permute-start.99 = (bf16[2,2,2,1,64,896]{5,4,3,2,1,0:T(8,128)(2,1)S(1)}, bf16[2,2,2,1,64,896]{5,4,3,2,1,0:T(8,128)(2,1)S(1)}, u32[]{:S(2)}, u32[]{:S(2)}) collective-permute-start(bf16[2,2,2,1,64,896]{5,4,3,2,1,0:T(8,128)(2,1)S(1)} %pad_maximum_fusion.8.refs_0_), channel_id=1, source_target_pairs={{0,24},{24,0},{8,16},{16,8},{1,25},{25,1},{9,17},{17,9},{2,26},{26... | collective-permute-start | bytes 2752520 | tf_op jit(solution)/shard_map/ppermute | solution.py:58
  360.5 14.2 %collective-permute-start.100 = (bf16[1,2,2,2,64,768]{5,4,3,2,1,0:T(8,128)(2,1)S(1)}, bf16[1,2,2,2,64,768]{5,4,3,2,1,0:T(8,128)(2,1)S(1)}, u32[]{:S(2)}, u32[]{:S(2)}) collective-permute-start(bf16[1,2,2,2,64,768]{5,4,3,2,1,0:T(8,128)(2,1)S(1)} %pad_maximum_fusion.16.refs_2_), channel_id=1, source_target_pairs={{0,32},{32,0},{64,96},{96,64},{1,33},{33,1},{65,97},{97,65},{2,34}... | collective-permute-start | bytes 2359304 | tf_op jit(solution)/shard_map/ppermute | solution.py:58
  361.7 13.6 %collective-permute-start.101 = (bf16[2,1,2,2,64,768]{5,4,3,2,1,0:T(8,128)(2,1)S(1)}, bf16[2,1,2,2,64,768]{5,4,3,2,1,0:T(8,128)(2,1)S(1)}, u32[]{:S(2)}, u32[]{:S(2)}) collective-permute-start(bf16[2,1,2,2,64,768]{5,4,3,2,1,0:T(8,128)(2,1)S(1)} %pad_maximum_fusion.17.refs_4_), channel_id=1, source_target_pairs={{0,8},{8,0},{16,24},{24,16},{1,9},{9,1},{17,25},{25,17},{2,10},{10... | collective-permute-start | bytes 2359304 | tf_op jit(solution)/shard_map/ppermute | solution.py:58
  361.8 14.8 %collective-permute-start.102 = (bf16[2,2,1,2,64,768]{5,4,3,2,1,0:T(8,128)(2,1)S(1)}, bf16[2,2,1,2,64,768]{5,4,3,2,1,0:T(8,128)(2,1)S(1)}, u32[]{:S(2)}, u32[]{:S(2)}) collective-permute-start(bf16[2,2,1,2,64,768]{5,4,3,2,1,0:T(8,128)(2,1)S(1)} %pad_maximum_fusion.18.refs_6_), channel_id=1, source_target_pairs={{0,96},{96,0},{32,64},{64,32},{1,97},{97,1},{33,65},{65,33},{2,98}... | collective-permute-start | bytes 2359304 | tf_op jit(solution)/shard_map/ppermute | solution.py:58
  (128 other events, 1461.2 us)
